TPU v7x, 32 devices: a whole 2x2x4 slice. The times are simulated.
32 devices in a mesh: dp: 4 (over z), expert: 8 (over y, x, core).
Axes of the slice: x: 2, y: 2, z: 4, core: 2. Of those that a mesh axis runs over, the one named last changes fastest.
Arguments:
- tokens: bfloat16 [1024, 3584], P('expert', 'dp'), may hold values from -6 to 6
- cotangent: bfloat16 [1024, 3584], P('expert', 'dp'), may hold values from -6 to 6
- routes: int32 [1024, 3], P('expert'), may hold values from 0 to 5, all different within a row; in each aligned block of 128 rows (0 to 127, 128 to 255, ...) at most 72 rows name the same one
- route_weight: float32 [1024, 3], P('expert'), may hold values from 0.1 to 0.6
- gate_weight: bfloat16 [8, 3584, 1024], P('expert', None, 'dp'), may hold values from -6 to 6
- up_weight: bfloat16 [8, 3584, 1024], P('expert', None, 'dp'), may hold values from -6 to 6
- down_weight: bfloat16 [8, 1024, 3584], P('expert', None, 'dp'), may hold values from -6 to 6
- first_moment: bfloat16 [8, 3584, 1024], P('expert', None, 'dp'), may hold values from -0.59765625 to 0.59765625
- second_moment: bfloat16 [8, 3584, 1024], P('expert', None, 'dp'), may hold values from 0.0009994507 to 0.029907227
- placement: int32 [8], replicated, may hold values from 0 to 5, as said below
- migration_plan: int32 [8], replicated, may hold values from 0 to 7, as said below
Outputs:
- layer_output: bfloat16 [1024, 3584], P('expert', 'dp')
- new_gate: bfloat16 [8, 3584, 1024], P('expert', None, 'dp')
- new_first: bfloat16 [8, 3584, 1024], P('expert', None, 'dp')
- new_second: bfloat16 [8, 3584, 1024], P('expert', None, 'dp')
Inputs may be any that keep to these rules, and one draw needn't show every extreme that they name: `routes`: each row names 3 different experts; among the rows of one index of the expert axis no expert is named more than 72 times. `placement`: every expert from 0 to 5 is held by one slot or more. `migration_plan`: every expert keeps one slot or more in the new placement.
All inputs are finite; a program needn't handle non-finite values.
Results may differ from a plain program's by a relative error of at most 0.033.
Values may be sent and summed in bfloat16 or wider, within the bound.
A program may use at most 128 MiB of HBM per device.

v0:
```python
import math

import jax
import jax.numpy as jnp
from jax import lax
from jax.sharding import PartitionSpec as P

D = 3584
FF = 1024


beta_first = 0.9
beta_second = 0.95
learn_rate = 0.02
weight_decay = 0.1
epsilon = 1e-08


def choose_slots(routes, placement, source):
    slot_iota = jnp.arange(placement.shape[0], dtype=jnp.int32)
    hosting = routes[..., None] == placement
    copies = jnp.sum(hosting, -1)
    earlier = (placement[:, None] == placement[None, :]) & (slot_iota[:, None] < slot_iota[None, :])
    replica_rank = jnp.sum(earlier, 0)
    replica = source[:, None] % copies
    matched = hosting & (replica_rank == replica[..., None])
    return jnp.sum(jnp.where(matched, slot_iota, 0), -1)


def place_rows(slot_ids, slot_count):
    tok_rows, per_token = slot_ids.shape
    flattened = slot_ids.reshape(-1)
    onehot = (flattened[:, None] == jnp.arange(slot_count, dtype=jnp.int32)).astype(jnp.int32)
    running = jnp.cumsum(onehot, 0)
    return (jnp.sum(running * onehot, 1) - 1).reshape(tok_rows, per_token)


def adam_update(gradient, weight, first_old, second):
    moment_one = beta_first * first_old.astype(jnp.float32) + (1.0 - beta_first) * gradient
    moment_two = (
        beta_second * second.astype(jnp.float32) + (1.0 - beta_second) * gradient * gradient
    )
    updated = weight.astype(jnp.float32) * (
        1.0 - learn_rate * weight_decay
    ) - learn_rate * moment_one / (jnp.sqrt(moment_two) + epsilon)
    return (
        updated.astype(jnp.bfloat16),
        moment_one.astype(jnp.bfloat16),
        moment_two.astype(jnp.bfloat16),
    )


def select_slots(selector, state):
    return jnp.einsum("st,tdf->sdf", selector, state, preferred_element_type=jnp.float32).astype(
        jnp.bfloat16
    )


def per_device(
    tokens,
    cotangent,
    routes,
    route_weight,
    gate_weight,
    up_weight,
    down_weight,
    first_moment,
    second_moment,
    placement,
    migration_plan,
):
    slot_count = lax.axis_size("expert")
    device_index = lax.axis_index("expert")
    tok_rows, quarter = tokens.shape
    per_token = routes.shape[1]
    capacity = min(tok_rows, 3 * tok_rows * per_token // (2 * slot_count))
    buffer_size = slot_count * capacity
    scale_in = 1.0 / math.sqrt(D)
    scale_mid = 1.0 / math.sqrt(FF)
    source = jnp.full((tok_rows,), device_index, jnp.int32)
    slot_ids = choose_slots(routes, placement, source)
    position = place_rows(slot_ids, slot_count)
    target = slot_ids * capacity + position
    buffer_slots = jnp.arange(buffer_size, dtype=jnp.int32)
    landing = target[None, :, :] == buffer_slots[:, None, None]
    selection = jnp.any(landing, -1).astype(jnp.bfloat16)
    row_weight = jnp.sum(jnp.where(landing, route_weight[None], jnp.float32(0.0)), (1, 2))
    sent_rows = jnp.dot(selection, tokens, preferred_element_type=jnp.float32).astype(jnp.bfloat16)
    picked_grads = jnp.dot(selection, cotangent, preferred_element_type=jnp.float32)
    sent_grads = (row_weight[:, None] * picked_grads).astype(jnp.bfloat16)
    sent_rows = sent_rows.reshape(slot_count, capacity, quarter)
    sent_grads = sent_grads.reshape(slot_count, capacity, quarter)
    got_rows, got_grads = (
        lax.all_to_all(sent_rows, "expert", split_axis=0, concat_axis=0, tiled=True),
        lax.all_to_all(sent_grads, "expert", split_axis=0, concat_axis=0, tiled=True),
    )
    inputs = lax.all_gather(got_rows.reshape(buffer_size, quarter), "dp", axis=1, tiled=True)
    gate_values = jnp.dot(inputs, gate_weight[0], preferred_element_type=jnp.float32) * scale_in
    up_values = jnp.dot(inputs, up_weight[0], preferred_element_type=jnp.float32) * scale_in
    hidden = (jax.nn.silu(gate_values) * up_values).astype(jnp.bfloat16)
    every_hidden = lax.all_gather(hidden, "dp", axis=1, tiled=True)
    w_down = down_weight[0]
    outputs = (
        jnp.dot(every_hidden, w_down, preferred_element_type=jnp.float32) * scale_mid
    ).astype(jnp.bfloat16)
    returned = lax.all_to_all(
        outputs.reshape(slot_count, capacity, quarter),
        "expert",
        split_axis=0,
        concat_axis=0,
        tiled=True,
    )
    returned_rows = returned.reshape(buffer_size, quarter)
    combined = jnp.zeros((tok_rows, quarter), jnp.float32)
    for route_index in range(per_token):
        rows_back = jnp.take(returned_rows, target[:, route_index], axis=0).astype(jnp.float32)
        combined = combined + route_weight[:, route_index : route_index + 1] * rows_back
    layer_output = combined.astype(jnp.bfloat16)
    partial_grad = lax.dot_general(
        got_grads.reshape(buffer_size, quarter),
        w_down,
        (((1,), (1,)), ((), ())),
        preferred_element_type=jnp.float32,
    )
    hidden_grad = (
        lax.psum_scatter(
            partial_grad.astype(jnp.bfloat16), "dp", scatter_dimension=1, tiled=True
        ).astype(jnp.float32)
        * scale_mid
    )
    sigmoid_gate = jax.nn.sigmoid(gate_values)
    gate_grad = (
        hidden_grad * up_values * sigmoid_gate * (1.0 + gate_values * (1.0 - sigmoid_gate))
    ).astype(jnp.bfloat16)
    weight_grad = (
        lax.dot_general(
            inputs, gate_grad, (((0,), (0,)), ((), ())), preferred_element_type=jnp.float32
        )
        * scale_in
    )
    same_expert = (placement[:, None] == placement[None, :]).astype(jnp.float32)
    selector = (migration_plan[:, None] == jnp.arange(slot_count, dtype=jnp.int32)[None, :]).astype(
        jnp.bfloat16
    )
    grad_parts = lax.all_to_all(
        weight_grad[None].astype(jnp.bfloat16), "expert", split_axis=1, concat_axis=0, tiled=True
    ).astype(jnp.float32)
    summed = jnp.einsum("st,tdf->sdf", same_expert, grad_parts, precision=lax.Precision.HIGHEST)
    state_parts = (
        lax.all_to_all(gate_weight, "expert", split_axis=1, concat_axis=0, tiled=True),
        lax.all_to_all(first_moment, "expert", split_axis=1, concat_axis=0, tiled=True),
        lax.all_to_all(second_moment, "expert", split_axis=1, concat_axis=0, tiled=True),
    )
    new_weight, new_one, new_two = adam_update(
        summed, state_parts[0], state_parts[1], state_parts[2]
    )
    migrated = (
        select_slots(selector, new_weight),
        select_slots(selector, new_one),
        select_slots(selector, new_two),
    )
    result = (
        lax.all_to_all(migrated[0], "expert", split_axis=0, concat_axis=1, tiled=True),
        lax.all_to_all(migrated[1], "expert", split_axis=0, concat_axis=1, tiled=True),
        lax.all_to_all(migrated[2], "expert", split_axis=0, concat_axis=1, tiled=True),
    )
    return (layer_output, result[0], result[1], result[2])


def solution(mesh):
    placed = (
        P("expert", "dp"),
        P("expert", "dp"),
        P("expert", None),
        P("expert", None),
        P("expert", None, "dp"),
        P("expert", None, "dp"),
        P("expert", None, "dp"),
        P("expert", None, "dp"),
        P("expert", None, "dp"),
        P(),
        P(),
    )
    return jax.shard_map(
        per_device,
        mesh=mesh,
        in_specs=placed,
        out_specs=(
            P("expert", "dp"),
            P("expert", None, "dp"),
            P("expert", None, "dp"),
            P("expert", None, "dp"),
        ),
        check_vma=False,
    )
```

profile of v0, /device:TPU:0, one launch (start us, length us, event | category | flops | bytes accessed | tf_op | source)
XLA Modules:
  0.0 400.9 jit_solution(13841018249110109182)
XLA Ops:
  13.3 20.3 %all_to_all.90 = bf16[8,72,896]{2,1,0:T(8,128)(2,1)} all-to-all(bf16[8,72,896]{2,1,0:T(8,128)(2,1)S(1)} %bitcast.108), channel_id=1, replica_groups=mesh['dp'=4,'expert'=8] {'expert'}, dimensions={0} | all-to-all | bytes 2064384 | tf_op jit(solution)/shard_map/all_to_all | solution.py:94
  38.8 6.9 %copy.117 = bf16[1,3584,256]{2,0,1:T(2,128)(2,1)} copy(bf16[1,3584,256]{2,1,0:T(8,128)(2,1)} %param.20) | data formatting | bytes 3670016 | tf_op args[7]
  46.2 20.3 %reduce.3 = bf16[3584,256]{1,0:T(8,128)(2,1)} reduce(bf16[3584,1,256]{2,1,0:T(2,128)(2,1)} %bitcast.101, bf16[]{:T(256)} %broadcast.107), dimensions={1}, to_apply=%bitcast.88.reduce_sub_computation | reduce | bytes 3670018
  66.5 5.7 %reshape.160 = bf16[8,2,57344]{2,1,0:T(2,128)(2,1)} reshape(bf16[3584,256]{1,0:T(8,128)(2,1)} %reduce.3) | data formatting | bytes 3670016
  76.5 6.8 %copy.115 = bf16[1,3584,256]{2,0,1:T(2,128)(2,1)} copy(bf16[1,3584,256]{2,1,0:T(8,128)(2,1)} %param.21) | data formatting | bytes 3670016 | tf_op args[8]
  83.3 20.3 %reduce.5 = bf16[3584,256]{1,0:T(8,128)(2,1)} reduce(bf16[3584,1,256]{2,1,0:T(2,128)(2,1)} %bitcast.104, bf16[]{:T(256)} %broadcast.107), dimensions={1}, to_apply=%bitcast.86.reduce_sub_computation | reduce | bytes 3670018
  103.6 5.7 %reshape.164 = bf16[8,2,57344]{2,1,0:T(2,128)(2,1)} reshape(bf16[3584,256]{1,0:T(8,128)(2,1)} %reduce.5) | data formatting | bytes 3670016
  116.4 6.8 %copy.118 = bf16[1,3584,256]{2,0,1:T(2,128)(2,1)} copy(bf16[1,3584,256]{2,1,0:T(8,128)(2,1)} %param.17) | data formatting | bytes 3670016 | tf_op args[4]
  123.2 20.3 %reduce.2 = bf16[3584,256]{1,0:T(8,128)(2,1)} reduce(bf16[3584,1,256]{2,1,0:T(2,128)(2,1)} %bitcast.105, bf16[]{:T(256)} %broadcast.107), dimensions={1}, to_apply=%bitcast.89.reduce_sub_computation | reduce | bytes 3670018
  143.6 5.7 %reshape.158 = bf16[8,2,57344]{2,1,0:T(2,128)(2,1)} reshape(bf16[3584,256]{1,0:T(8,128)(2,1)} %reduce.2) | data formatting | bytes 3670016
  149.3 6.7 %reshape.161 = bf16[3584,1,256]{2,1,0:T(2,128)(2,1)} reshape(bf16[8,2,57344]{2,1,0:T(2,128)(2,1)} %all-to-all-done.3) | data formatting | bytes 3670016
  164.6 6.7 %reshape.165 = bf16[3584,1,256]{2,1,0:T(2,128)(2,1)} reshape(bf16[8,2,57344]{2,1,0:T(2,128)(2,1)} %all-to-all-done.6) | data formatting | bytes 3670016
  181.8 22.0 %copy.116 = bf16[1,3584,256]{2,0,1:T(2,128)(2,1)} copy(bf16[1,3584,256]{2,1,0:T(8,128)(2,1)S(1)} %fusion.1) | data formatting | bytes 3670016 | tf_op jit(solution)/shard_map/convert_element_type | solution.py:146
  203.8 20.3 %reduce.4 = bf16[3584,256]{1,0:T(8,128)(2,1)} reduce(bf16[3584,1,256]{2,1,0:T(2,128)(2,1)} %bitcast.102, bf16[]{:T(256)} %broadcast.107), dimensions={1}, to_apply=%bitcast.87.reduce_sub_computation | reduce | bytes 3670018
  224.1 5.7 %reshape.162 = bf16[8,2,57344]{2,1,0:T(2,128)(2,1)} reshape(bf16[3584,256]{1,0:T(8,128)(2,1)} %reduce.4) | data formatting | bytes 3670016
  229.8 12.9 %all-to-all-start.5 = ((bf16[8,2,57344]{2,1,0:T(2,128)(2,1)}), bf16[8,2,57344]{2,1,0:T(2,128)(2,1)}, u32[]{:S(2)}, u32[]{:S(2)}) async-start(bf16[8,2,57344]{2,1,0:T(2,128)(2,1)} %reshape.162), calls=%async_computation.6 | async-start | bytes 3670016 | tf_op jit(solution)/shard_map/all_to_all | solution.py:145
  247.0 6.6 %reshape.159 = bf16[3584,1,256]{2,1,0:T(2,128)(2,1)} reshape(bf16[8,2,57344]{2,1,0:T(2,128)(2,1)} %all-to-all-done.2) | data formatting | bytes 3670016
  258.0 8.4 %all-to-all-done.5 = bf16[8,2,57344]{2,1,0:T(2,128)(2,1)} async-done(((bf16[8,2,57344]{2,1,0:T(2,128)(2,1)}), bf16[8,2,57344]{2,1,0:T(2,128)(2,1)}, u32[]{:S(2)}, u32[]{:S(2)}) %all-to-all-start.5) | async-done | bytes 1835040 | tf_op jit(solution)/shard_map/all_to_all | solution.py:145
  266.4 6.6 %reshape.163 = bf16[3584,1,256]{2,1,0:T(2,128)(2,1)} reshape(bf16[8,2,57344]{2,1,0:T(2,128)(2,1)} %all-to-all-done.5) | data formatting | bytes 3670016
  285.7 12.1 %fusion.20 = bf16[8,448,256]{2,0,1:T(8,128)(2,1)S(1)} fusion(f32[8,448,256]{2,1,0:T(8,128)} %bitcast.109, f32[8,448,256]{2,1,0:T(8,128)} %bitcast.94, f32[8,448,256]{2,0,1:T(8,128)} %fusion.12, f32[8,448,256]{2,1,0:T(8,128)} %bitcast.96, s32[8]{0:T(128)S(1)} %copy-done.4), kind=kOutput, calls=%fused_computation.31 | convolution fusion | flops 24772672 | bytes 16515104 | tf_op jit(solution)/shard_map/st,tdf->sdf/dot_general | solution.py:54
  312.5 16.8 %all-to-all-done.7 = bf16[8,448,256]{2,1,0:T(8,128)(2,1)} async-done(((bf16[8,448,256]{2,1,0:T(8,128)(2,1)}), bf16[8,448,256]{2,1,0:T(8,128)(2,1)}, u32[]{:S(2)}, u32[]{:S(2)}) %all-to-all-start.7) | async-done | bytes 1835040 | tf_op jit(solution)/shard_map/all_to_all | solution.py:163
  333.6 5.5 %fusion.26 = bf16[8,448,256]{2,0,1:T(8,128)(2,1)S(1)} fusion(f32[8,448,256]{2,0,1:T(8,128)} %fusion.12, f32[8,448,256]{2,1,0:T(8,128)} %bitcast.97, s32[8]{0:T(128)S(1)} %copy-done.4), kind=kOutput, calls=%fused_computation.33 | convolution fusion | flops 19267648 | bytes 9175072 | tf_op jit(solution)/shard_map/st,tdf->sdf/dot_general | solution.py:54
  340.7 16.8 %all-to-all-done.8 = bf16[8,448,256]{2,1,0:T(8,128)(2,1)} async-done(((bf16[8,448,256]{2,1,0:T(8,128)(2,1)}), bf16[8,448,256]{2,1,0:T(8,128)(2,1)}, u32[]{:S(2)}, u32[]{:S(2)}) %all-to-all-start.8) | async-done | bytes 1835040 | tf_op jit(solution)/shard_map/all_to_all | solution.py:164
  367.9 17.7 %all-to-all-done.9 = bf16[8,448,256]{2,1,0:T(8,128)(2,1)} async-done(((bf16[8,448,256]{2,1,0:T(8,128)(2,1)}), bf16[8,448,256]{2,1,0:T(8,128)(2,1)}, u32[]{:S(2)}, u32[]{:S(2)}) %all-to-all-start.9) | async-done | bytes 1835040 | tf_op jit(solution)/shard_map/all_to_all | solution.py:165
  (82 shorter events, 103.2 us)
Async XLA Ops:
  7.2 106.8 %copy-start = (bf16[1,1024,896]{2,1,0:T(8,128)(2,1)S(1)}, bf16[1,1024,896]{2,1,0:T(8,128)(2,1)}, u32[]{:S(2)}) copy-start(bf16[1,1024,896]{2,1,0:T(8,128)(2,1)} %param.19) | copy-start | bytes 5505028
  7.2 26.5 %copy-start.3 = (f32[128,3]{0,1:T(4,128)S(1)}, f32[128,3]{0,1:T(4,128)}, u32[]{:S(2)}) copy-start(f32[128,3]{0,1:T(4,128)} %param.16) | copy-start | bytes 4612
  7.2 26.6 %copy-start.1 = (bf16[128,896]{1,0:T(8,128)(2,1)S(1)}, bf16[128,896]{1,0:T(8,128)(2,1)}, u32[]{:S(2)}) copy-start(bf16[128,896]{1,0:T(8,128)(2,1)} %param.14) | copy-start | bytes 688132
  7.2 164.0 %all-gather.3.cloned.1.call-start = ((), (), s32[]{:S(2)}) async-start(), calls=%async_computation.11 | async-start | bytes 5160960 | tf_op jit(solution)/shard_map/all_gather | solution.py:97
  35.2 37.0 %all-to-all-start.4 = ((bf16[8,72,896]{2,1,0:T(8,128)(2,1)}), bf16[8,72,896]{2,1,0:T(8,128)(2,1)S(1)}, u32[]{:S(2)}, u32[]{:S(2)}) async-start(bf16[8,72,896]{2,1,0:T(8,128)(2,1)} %bitcast.19), calls=%async_computation.4 | async-start | bytes 2064384 | tf_op jit(solution)/shard_map/all_to_all | solution.py:95
  72.2 37.1 %all-to-all-start.3 = ((bf16[8,2,57344]{2,1,0:T(2,128)(2,1)}), bf16[8,2,57344]{2,1,0:T(2,128)(2,1)}, u32[]{:S(2)}, u32[]{:S(2)}) async-start(bf16[8,2,57344]{2,1,0:T(2,128)(2,1)} %reshape.160), calls=%async_computation.3 | async-start | bytes 3670016 | tf_op jit(solution)/shard_map/all_to_all | solution.py:151
  109.3 46.6 %all-to-all-start.6 = ((bf16[8,2,57344]{2,1,0:T(2,128)(2,1)}), bf16[8,2,57344]{2,1,0:T(2,128)(2,1)}, u32[]{:S(2)}, u32[]{:S(2)}) async-start(bf16[8,2,57344]{2,1,0:T(2,128)(2,1)} %reshape.164), calls=%async_computation.7 | async-start | bytes 3670016 | tf_op jit(solution)/shard_map/all_to_all | solution.py:152
  113.7 64.1 %reduce-scatter.2.cloned.1.call-start = ((), (), s32[]{:S(2)}) async-start(), calls=%async_computation.13 | async-start | bytes 1474560 | tf_op jit(solution)/shard_map/reduce_scatter | solution.py:126
  155.9 73.9 %all-to-all-start.2 = ((bf16[8,2,57344]{2,1,0:T(2,128)(2,1)}), bf16[8,2,57344]{2,1,0:T(2,128)(2,1)}, u32[]{:S(2)}, u32[]{:S(2)}) async-start(bf16[8,2,57344]{2,1,0:T(2,128)(2,1)} %reshape.158), calls=%async_computation.2 | async-start | bytes 3670016 | tf_op jit(solution)/shard_map/all_to_all | solution.py:150
  160.2 118.3 %all-gather.5.cloned.1.call-start = ((), (), s32[]{:S(2)}) async-start(), calls=%async_computation.12 | async-start | bytes 1474560 | tf_op jit(solution)/shard_map/all_gather | solution.py:101
  171.2 4.1 %copy-start.5 = (bf16[576,3584]{1,0:T(8,128)(2,1)S(1)}, bf16[576,3584]{1,0:T(8,128)(2,1)}, u32[]{:S(2)}) copy-start(bf16[576,3584]{1,0:T(8,128)(2,1)} %all-gather.3.cloned.1.call-done) | copy-start | bytes 12386308
  171.2 4.5 %copy-start.6 = (bf16[1,3584,256]{2,1,0:T(8,128)(2,1)S(1)}, bf16[1,3584,256]{2,1,0:T(8,128)(2,1)}, u32[]{:S(2)}) copy-start(bf16[1,3584,256]{2,1,0:T(8,128)(2,1)} %param.18) | copy-start | bytes 5505028
  229.8 36.6 %all-to-all-start.5 = ((bf16[8,2,57344]{2,1,0:T(2,128)(2,1)}), bf16[8,2,57344]{2,1,0:T(2,128)(2,1)}, u32[]{:S(2)}, u32[]{:S(2)}) async-start(bf16[8,2,57344]{2,1,0:T(2,128)(2,1)} %reshape.162), calls=%async_computation.6 | async-start | bytes 3670016 | tf_op jit(solution)/shard_map/all_to_all | solution.py:145
  273.0 2.4 copy-start.2
  278.5 7.2 %copy-start.4 = (s32[8]{0:T(128)S(1)}, s32[8]{0:T(128)}, u32[]{:S(2)}) copy-start(s32[8]{0:T(128)} %param.23) | copy-start | bytes 100
  282.1 18.7 %all-to-all-start.1 = ((bf16[8,72,896]{2,1,0:T(8,128)(2,1)}), bf16[8,72,896]{2,1,0:T(8,128)(2,1)S(1)}, u32[]{:S(2)}, u32[]{:S(2)}) async-start(bf16[8,72,896]{2,1,0:T(8,128)(2,1)} %bitcast.111), calls=%async_computation.1 | async-start | bytes 2064384 | tf_op jit(solution)/shard_map/all_to_all | solution.py:106
  300.9 28.4 %all-to-all-start.7 = ((bf16[8,448,256]{2,1,0:T(8,128)(2,1)}), bf16[8,448,256]{2,1,0:T(8,128)(2,1)}, u32[]{:S(2)}, u32[]{:S(2)}) async-start(bf16[8,448,256]{2,1,0:T(8,128)(2,1)} %copy.82), calls=%async_computation.8 | async-start | bytes 3670016 | tf_op jit(solution)/shard_map/all_to_all | solution.py:163
  329.3 28.2 %all-to-all-start.8 = ((bf16[8,448,256]{2,1,0:T(8,128)(2,1)}), bf16[8,448,256]{2,1,0:T(8,128)(2,1)}, u32[]{:S(2)}, u32[]{:S(2)}) async-start(bf16[8,448,256]{2,1,0:T(8,128)(2,1)} %copy.83), calls=%async_computation.9 | async-start | bytes 3670016 | tf_op jit(solution)/shard_map/all_to_all | solution.py:164
  357.4 28.2 %all-to-all-start.9 = ((bf16[8,448,256]{2,1,0:T(8,128)(2,1)}), bf16[8,448,256]{2,1,0:T(8,128)(2,1)}, u32[]{:S(2)}, u32[]{:S(2)}) async-start(bf16[8,448,256]{2,1,0:T(8,128)(2,1)} %copy.84), calls=%async_computation.10 | async-start | bytes 3670016 | tf_op jit(solution)/shard_map/all_to_all | solution.py:165
Sparse Core Ops, SparseCore 0:
  33.8 79.0 all-gather.2
  116.8 30.7 reduce-scatter.1
  177.8 33.3 all-gather.4
where the time goes:
time: 406 us; the launch traced here: 401 us
  local copies, waits for them, and re-layouts  113 us (28%)
  other arithmetic  101 us (25%)
  waiting for transfers between devices  61.2 us (15%)
  starting transfers between devices  46.5 us (11%)
  matrix products  45.1 us (11%)
  blocking collectives  20.3 us (5%)
  between operations  14.2 us (3%)
    unnamed x30, local copies, waits for them, and re-layouts  81.6 us
    unnamed x4, other arithmetic  81.3 us
    dot_general x3, matrix products, select_slots(): jnp.einsum('st,tdf->sdf', selector, state, preferred_element_type=jnp.flo...  23.1 us
    convert_element_type x1, local copies, waits for them, and re-layouts, per_device(): weight_grad[None].astype(jnp.bfloat16)  22 us
    all_to_all x1, blocking collectives, per_device(): lax.all_to_all(sent_rows, 'expert', split_axis=0, concat_axis=0, tiled=True)  20.3 us
    all_to_all x1, waiting for transfers between devices, per_device(): lax.all_to_all(migrated[2], 'expert', split_axis=0, concat_axis=1, tiled=...  17.7 us
    all_to_all x1, waiting for transfers between devices, per_device(): lax.all_to_all(migrated[0], 'expert', split_axis=0, concat_axis=1, tiled=...  16.8 us
    all_to_all x1, waiting for transfers between devices, per_device(): lax.all_to_all(migrated[1], 'expert', split_axis=0, concat_axis=1, tiled=...  16.8 us
  transfers between devices with their start and end apart: 12, of which 5 were waited for; matrix products, arithmetic and copies ran while one was open for 60% of the time, Pallas kernels for 0%

commit v1 on v0

--- a/solution.py
+++ b/solution.py
@@ -3,6 +3,8 @@
 import jax
 import jax.numpy as jnp
 from jax import lax
+from jax.experimental import pallas as pl
+from jax.experimental.pallas import tpu as pltpu
 from jax.sharding import PartitionSpec as P
 
 D = 3584
@@ -31,7 +33,12 @@
     tok_rows, per_token = slot_ids.shape
     flattened = slot_ids.reshape(-1)
     onehot = (flattened[:, None] == jnp.arange(slot_count, dtype=jnp.int32)).astype(jnp.int32)
-    running = jnp.cumsum(onehot, 0)
+    count = flattened.shape[0]
+    order = jnp.arange(count, dtype=jnp.int32)
+    upto = (order[:, None] >= order[None, :]).astype(jnp.bfloat16)
+    running = jnp.dot(
+        upto, onehot.astype(jnp.bfloat16), preferred_element_type=jnp.float32
+    ).astype(jnp.int32)
     return (jnp.sum(running * onehot, 1) - 1).reshape(tok_rows, per_token)
 
 
@@ -50,10 +57,44 @@
     )
 
 
-def select_slots(selector, state):
-    return jnp.einsum("st,tdf->sdf", selector, state, preferred_element_type=jnp.float32).astype(
-        jnp.bfloat16
-    )
+def update_kernel(
+    placement_ref, plan_ref, weight_ref, first_ref, second_ref, grad_ref, out_w, out_1, out_2
+):
+    held = placement_ref[plan_ref[pl.program_id(0)]]
+    slots, rows, _ = grad_ref.shape
+    chunk = math.gcd(rows, 112)
+
+    @pl.loop(0, rows // chunk)
+    def _(step):
+        part = pl.ds(pl.multiple_of(step * chunk, chunk), chunk)
+        gradient = jnp.zeros((chunk, grad_ref.shape[2]), jnp.float32)
+        for slot in range(slots):
+            share = jnp.where(placement_ref[slot] == held, 1.0, 0.0).astype(jnp.float32)
+            gradient = gradient + share * grad_ref[slot, part].astype(jnp.float32)
+        out_w[0, part], out_1[0, part], out_2[0, part] = adam_update(
+            gradient, weight_ref[0, part], first_ref[0, part], second_ref[0, part]
+        )
+
+
+def update_slots(placement, plan, weight, first, second, grads):
+    slots, rows, columns = weight.shape
+    taken = pl.BlockSpec((1, rows, columns), lambda s, held, plan: (plan[s], 0, 0))
+    every = pl.BlockSpec((slots, rows, columns), lambda s, held, plan: (0, 0, 0))
+    made = pl.BlockSpec((1, rows, columns), lambda s, held, plan: (s, 0, 0))
+    return pl.pallas_call(
+        update_kernel,
+        out_shape=[jax.ShapeDtypeStruct(weight.shape, jnp.bfloat16)] * 3,
+        grid_spec=pltpu.PrefetchScalarGridSpec(
+            num_scalar_prefetch=2,
+            grid=(slots,),
+            in_specs=[taken, taken, taken, every],
+            out_specs=[made, made, made],
+        ),
+        compiler_params=pltpu.CompilerParams(vmem_limit_bytes=32 * 2**20),
+        cost_estimate=pl.CostEstimate(
+            flops=30 * weight.size, bytes_accessed=14 * weight.size, transcendentals=weight.size
+        ),
+    )(placement, plan, weight, first, second, grads)
 
 
 def per_device(
@@ -138,32 +179,19 @@
         )
         * scale_in
     )
-    same_expert = (placement[:, None] == placement[None, :]).astype(jnp.float32)
-    selector = (migration_plan[:, None] == jnp.arange(slot_count, dtype=jnp.int32)[None, :]).astype(
-        jnp.bfloat16
-    )
-    grad_parts = lax.all_to_all(
-        weight_grad[None].astype(jnp.bfloat16), "expert", split_axis=1, concat_axis=0, tiled=True
-    ).astype(jnp.float32)
-    summed = jnp.einsum("st,tdf->sdf", same_expert, grad_parts, precision=lax.Precision.HIGHEST)
-    state_parts = (
-        lax.all_to_all(gate_weight, "expert", split_axis=1, concat_axis=0, tiled=True),
-        lax.all_to_all(first_moment, "expert", split_axis=1, concat_axis=0, tiled=True),
-        lax.all_to_all(second_moment, "expert", split_axis=1, concat_axis=0, tiled=True),
-    )
-    new_weight, new_one, new_two = adam_update(
-        summed, state_parts[0], state_parts[1], state_parts[2]
-    )
-    migrated = (
-        select_slots(selector, new_weight),
-        select_slots(selector, new_one),
-        select_slots(selector, new_two),
-    )
-    result = (
-        lax.all_to_all(migrated[0], "expert", split_axis=0, concat_axis=1, tiled=True),
-        lax.all_to_all(migrated[1], "expert", split_axis=0, concat_axis=1, tiled=True),
-        lax.all_to_all(migrated[2], "expert", split_axis=0, concat_axis=1, tiled=True),
-    )
+    def exchange(array):
+        split = array.reshape(slot_count, array.shape[-2] // slot_count, array.shape[-1])
+        return lax.all_to_all(split, "expert", split_axis=0, concat_axis=0, tiled=True)
+
+    state_parts = [exchange(array[0]) for array in (gate_weight, first_moment, second_moment)]
+    grad_parts = exchange(weight_grad.astype(jnp.bfloat16))
+    updated = update_slots(placement, migration_plan, *state_parts, grad_parts)
+    result = [
+        lax.all_to_all(array, "expert", split_axis=0, concat_axis=0, tiled=True).reshape(
+            first_moment.shape
+        )
+        for array in updated
+    ]
     return (layer_output, result[0], result[1], result[2])
 
 

time: 406 us -> 296 us (0.73)
  blocking collectives: 20.3 us -> 120 us
  local copies, waits for them, and re-layouts: 113 us -> 16.6 us
  other arithmetic: 101 us -> 5.68 us
  waiting for transfers between devices: 61.2 us -> 88.2 us
  matrix products: 45.1 us -> 19.4 us
  starting transfers between devices: 46.5 us -> 21.1 us
  Pallas kernels: 0 us -> 9.45 us
    all_to_all x0 -> x4, blocking collectives: none -> 99.7 us  [the longest x2 55.2 us: per_device(): lax.all_to_all(array, 'expert', split_axis=0, concat_axis=0, tiled=True)]
    unnamed x4 -> x0, other arithmetic: 81.3 us -> none
    unnamed x30 -> x31, local copies, waits for them, and re-layouts: 81.6 us -> 12.7 us
    convert_element_type x4 -> x0, local copies, waits for them, and re-layouts: 26.8 us -> none  [the longest x1 22 us: per_device(): weight_grad[None].astype(jnp.bfloat16)]
    dot_general x4 -> x1, matrix products: 26.2 us -> 0.21 us  [place_rows(): jnp.dot(upto, onehot.astype(jnp.bfloat16), preferred_element_type=jnp.flo...]
    all_to_all x8 -> x4, starting transfers between devices: 42.5 us -> 17.3 us  [the longest x3 13 us: exchange(): lax.all_to_all(split, 'expert', split_axis=0, concat_axis=0, tiled=True)]
    reduce_scatter x1, waiting for transfers between devices: 0.02 us -> 24.1 us  [per_device(): lax.psum_scatter(partial_grad.astype(jnp.bfloat16), 'dp', scatter_dimensi...]
    all_gather x1, waiting for transfers between devices: 0.01 us -> 23 us  [per_device(): every_hidden = lax.all_gather(hidden, 'dp', axis=1, tiled=True)]
  transfers between devices with their start and end apart: 12 -> 8, of which waited for: 5 -> 6; matrix products, arithmetic and copies ran while one was open for 60% -> 8% of each run, Pallas kernels for 0% -> 3%
where the time goes in v1:
time: 296 us; the launch traced here: 295 us
  blocking collectives  120 us (41%)
  waiting for transfers between devices  88.2 us (30%)
  starting transfers between devices  21.1 us (7%)
  matrix products  19.4 us (7%)
  local copies, waits for them, and re-layouts  16.6 us (6%)
  between operations  14 us (5%)
  Pallas kernels  9.45 us (3%)
  other arithmetic  5.68 us (2%)
    all_to_all x2, blocking collectives, per_device(): lax.all_to_all(array, 'expert', split_axis=0, concat_axis=0, tiled=True)  55.2 us
    all_to_all x1, blocking collectives, exchange(): lax.all_to_all(split, 'expert', split_axis=0, concat_axis=0, tiled=True)  26.9 us
    reduce_scatter x1, waiting for transfers between devices, per_device(): lax.psum_scatter(partial_grad.astype(jnp.bfloat16), 'dp', scatter_dimensi...  24.1 us
    all_gather x1, waiting for transfers between devices, per_device(): every_hidden = lax.all_gather(hidden, 'dp', axis=1, tiled=True)  23 us
    all_to_all x3, waiting for transfers between devices, exchange(): lax.all_to_all(split, 'expert', split_axis=0, concat_axis=0, tiled=True)  21.3 us
    all_to_all x1, blocking collectives, per_device(): lax.all_to_all(sent_rows, 'expert', split_axis=0, concat_axis=0, tiled=True)  20.4 us
    all_to_all x1, waiting for transfers between devices, per_device(): lax.all_to_all(array, 'expert', split_axis=0, concat_axis=0, tiled=True)  17.7 us
    all_to_all x1, blocking collectives, per_device(): lax.all_to_all(sent_grads, 'expert', split_axis=0, concat_axis=0, tiled=T...  17.6 us
  transfers between devices with their start and end apart: 8, of which 6 were waited for; matrix products, arithmetic and copies ran while one was open for 8% of the time, Pallas kernels for 3%

profile of v1, /device:TPU:0, one launch (start us, length us, event | category | flops | bytes accessed | tf_op | source)
XLA Modules:
  0.0 294.5 jit_solution(9791317066486499856)
XLA Ops:
  12.1 20.4 %all_to_all.50 = bf16[8,72,896]{2,1,0:T(8,128)(2,1)} all-to-all(bf16[8,72,896]{2,1,0:T(8,128)(2,1)S(1)} %bitcast.65), channel_id=1, replica_groups=mesh['dp'=4,'expert'=8] {'expert'}, dimensions={0} | all-to-all | bytes 2064384 | tf_op jit(solution)/shard_map/all_to_all | solution.py:135
  33.2 17.6 %all_to_all.51 = bf16[8,72,896]{2,1,0:T(8,128)(2,1)S(1)} all-to-all(bf16[8,72,896]{2,1,0:T(8,128)(2,1)S(1)} %bitcast.64), channel_id=1, replica_groups=mesh['dp'=4,'expert'=8] {'expert'}, dimensions={0} | all-to-all | bytes 2064384 | tf_op jit(solution)/shard_map/all_to_all | solution.py:136
  50.8 26.9 %all_to_all.52.weight_ref = bf16[8,448,256]{2,1,0:T(8,128)(2,1)} all-to-all(bf16[8,448,256]{2,1,0:T(8,128)(2,1)S(1)} %bitcast.67), channel_id=1, replica_groups=mesh['dp'=4,'expert'=8] {'expert'}, dimensions={0} | all-to-all | bytes 3670016 | tf_op jit(solution)/shard_map/all_to_all | solution.py:184
  77.7 4.3 %all-to-all-start.3 = ((bf16[8,448,256]{2,1,0:T(8,128)(2,1)}), bf16[8,448,256]{2,1,0:T(8,128)(2,1)}, u32[]{:S(2)}, u32[]{:S(2)}) async-start(bf16[8,448,256]{2,1,0:T(8,128)(2,1)} %bitcast.66), calls=%async_computation.3 | async-start | bytes 3670016 | tf_op jit(solution)/shard_map/all_to_all | solution.py:184
  82.1 2.4 fusion.9
  84.6 21.3 %all-to-all-done.3.first_ref = bf16[8,448,256]{2,1,0:T(8,128)(2,1)} async-done(((bf16[8,448,256]{2,1,0:T(8,128)(2,1)}), bf16[8,448,256]{2,1,0:T(8,128)(2,1)}, u32[]{:S(2)}, u32[]{:S(2)}) %all-to-all-start.3) | async-done | bytes 1835040 | tf_op jit(solution)/shard_map/all_to_all | solution.py:184
  105.9 4.3 %all-to-all-start.4 = ((bf16[8,448,256]{2,1,0:T(8,128)(2,1)}), bf16[8,448,256]{2,1,0:T(8,128)(2,1)}, u32[]{:S(2)}, u32[]{:S(2)}) async-start(bf16[8,448,256]{2,1,0:T(8,128)(2,1)} %bitcast.68), calls=%async_computation.4 | async-start | bytes 3670016 | tf_op jit(solution)/shard_map/all_to_all | solution.py:184
  111.7 4.1 %fusion.14 = f32[576,256]{1,0:T(8,128)S(1)} fusion(bf16[576,3584]{1,0:T(8,128)(2,1)} %all-gather.3.cloned.1.call-done, bf16[1,3584,256]{2,1,0:T(8,128)(2,1)} %param.17), kind=kOutput, calls=%fused_computation.17 | convolution fusion | flops 1057112064 | bytes 6553600 | tf_op jit(solution)/shard_map/dot_general | solution.py:139
  116.3 1.9 multiply_convert_fusion.3
  118.2 24.1 %reduce-scatter.2.cloned.1.call-done = bf16[576,256]{1,0:T(8,128)(2,1)} async-done(((bf16[576,1024]{1,0:T(8,128)(2,1)}), bf16[576,256]{1,0:T(8,128)(2,1)}) %reduce-scatter.2.cloned.1.call-update) | async-done | bytes 294928 | tf_op jit(solution)/shard_map/reduce_scatter | solution.py:167
  142.4 5.3 %fusion = bf16[3584,256]{1,0:T(8,128)(2,1)} fusion(bf16[576,3584]{1,0:T(8,128)(2,1)} %all-gather.3.cloned.1.call-done, f32[576,256]{1,0:T(8,128)S(1)} %fusion.14, f32[576,256]{1,0:T(8,128)S(1)} %get-tuple-element.25, bf16[576,256]{1,0:T(8,128)(2,1)} %reduce-scatter.2.cloned.1.call-done), kind=kOutput, calls=%fused_computation.4 | convolution fusion | flops 1060569088 | bytes 7438336 | tf_op jit(solution)/shard_map/dot_general | solution.py:177
  147.6 4.3 %all-to-all-start.6 = ((bf16[8,448,256]{2,1,0:T(8,128)(2,1)}), bf16[8,448,256]{2,1,0:T(8,128)(2,1)}, u32[]{:S(2)}, u32[]{:S(2)}) async-start(bf16[8,448,256]{2,1,0:T(8,128)(2,1)} %bitcast.69), calls=%async_computation.7 | async-start | bytes 3670016 | tf_op jit(solution)/shard_map/all_to_all | solution.py:184
  152.0 23.0 %all-gather.5.cloned.1.call-done = bf16[576,1024]{1,0:T(8,128)(2,1)} async-done(((bf16[576,256]{1,0:T(8,128)(2,1)}), bf16[576,1024]{1,0:T(8,128)(2,1)}) %all-gather.5.cloned.1.call-update) | async-done | bytes 1179664 | tf_op jit(solution)/shard_map/all_gather | solution.py:142
  175.0 3.6 %multiply_convert_fusion.1 = bf16[576,896]{1,0:T(8,128)(2,1)} fusion(bf16[576,1024]{1,0:T(8,128)(2,1)} %all-gather.5.cloned.1.call-done, bf16[1,1024,896]{2,1,0:T(8,128)(2,1)S(1)} %copy-done), kind=kOutput, calls=%fused_computation.6 | convolution fusion | flops 1057996800 | bytes 4046848 | tf_op jit(solution)/shard_map/dot_general | solution.py:145
  178.7 3.7 %all-to-all-start.1 = ((bf16[8,72,896]{2,1,0:T(8,128)(2,1)}), bf16[8,72,896]{2,1,0:T(8,128)(2,1)S(1)}, u32[]{:S(2)}, u32[]{:S(2)}) async-start(bf16[8,72,896]{2,1,0:T(8,128)(2,1)} %bitcast.70), calls=%async_computation.1 | async-start | bytes 2064384 | tf_op jit(solution)/shard_map/all_to_all | solution.py:147
  182.4 1.5 copy-done.1
  183.9 9.5 %shard_map.138 = (bf16[8,448,256]{2,1,0:T(8,128)(2,1)S(1)}, bf16[8,448,256]{2,1,0:T(8,128)(2,1)S(1)}, bf16[8,448,256]{2,1,0:T(8,128)(2,1)S(1)}) custom-call(s32[8]{0:T(128)S(1)} %copy-done.6, s32[8]{0:T(128)S(1)} %copy-done.7, bf16[8,448,256]{2,1,0:T(8,128)(2,1)S(1)} %copy-done.1, bf16[8,448,256]{2,1,0:T(8,128)(2,1)} %all-to-all-done.3.first_ref, ...), custom_call_target="tpu_custom_call" | custom-call | flops 27525120 | bytes 12845056 | tf_op jit(solution)/shard_map/pallas_call | solution.py:84
  197.6 28.3 %all_to_all.53 = bf16[8,448,256]{2,1,0:T(8,128)(2,1)} all-to-all(bf16[8,448,256]{2,1,0:T(8,128)(2,1)} %copy-done.5), channel_id=1, replica_groups=mesh['dp'=4,'expert'=8] {'expert'}, dimensions={0} | all-to-all | bytes 3670016 | tf_op jit(solution)/shard_map/all_to_all | solution.py:190
  225.8 26.9 %all_to_all.54 = bf16[8,448,256]{2,1,0:T(8,128)(2,1)} all-to-all(bf16[8,448,256]{2,1,0:T(8,128)(2,1)S(1)} %copy-done.4), channel_id=1, replica_groups=mesh['dp'=4,'expert'=8] {'expert'}, dimensions={0} | all-to-all | bytes 3670016 | tf_op jit(solution)/shard_map/all_to_all | solution.py:190
  252.8 4.3 %all-to-all-start.9 = ((bf16[8,448,256]{2,1,0:T(8,128)(2,1)}), bf16[8,448,256]{2,1,0:T(8,128)(2,1)}, u32[]{:S(2)}, u32[]{:S(2)}) async-start(bf16[8,448,256]{2,1,0:T(8,128)(2,1)} %copy-done.2), calls=%async_computation.10 | async-start | bytes 3670016 | tf_op jit(solution)/shard_map/all_to_all | solution.py:190
  261.6 1.6 add_convert_fusion
  263.2 17.7 %all-to-all-done.9 = bf16[8,448,256]{2,1,0:T(8,128)(2,1)} async-done(((bf16[8,448,256]{2,1,0:T(8,128)(2,1)}), bf16[8,448,256]{2,1,0:T(8,128)(2,1)}, u32[]{:S(2)}, u32[]{:S(2)}) %all-to-all-start.9) | async-done | bytes 1835040 | tf_op jit(solution)/shard_map/all_to_all | solution.py:190
  280.9 3.0 %copy.27 = bf16[1,3584,256]{2,1,0:T(8,128)(2,1)} copy(bf16[1,3584,256]{2,1,0:T(8,128)(2,1)} %bitcast.61) | data formatting | bytes 3670016
  285.1 2.8 copy.29
  (60 shorter events, 17.4 us)
Async XLA Ops:
  7.2 74.9 %copy-start = (bf16[1,1024,896]{2,1,0:T(8,128)(2,1)S(1)}, bf16[1,1024,896]{2,1,0:T(8,128)(2,1)}, u32[]{:S(2)}) copy-start(bf16[1,1024,896]{2,1,0:T(8,128)(2,1)} %param.19) | copy-start | bytes 5505028
  7.2 104.6 %all-gather.3.cloned.1.call-start = ((), (), s32[]{:S(2)}) async-start(), calls=%async_computation.11 | async-start | bytes 5160960 | tf_op jit(solution)/shard_map/all_gather | solution.py:138
  12.1 20.4 %copy-start.11 = (f32[128,3]{0,1:T(4,128)S(1)}, f32[128,3]{0,1:T(4,128)}, u32[]{:S(2)}) copy-start(f32[128,3]{0,1:T(4,128)} %param.16) | copy-start | bytes 4612
  12.1 20.6 %copy-start.10 = (bf16[128,896]{1,0:T(8,128)(2,1)S(1)}, bf16[128,896]{1,0:T(8,128)(2,1)}, u32[]{:S(2)}) copy-start(bf16[128,896]{1,0:T(8,128)(2,1)} %param.14) | copy-start | bytes 688132
  32.5 18.3 %copy-start.9 = (bf16[1,3584,256]{2,1,0:T(8,128)(2,1)S(1)}, bf16[1,3584,256]{2,1,0:T(8,128)(2,1)}, u32[]{:S(2)}) copy-start(bf16[1,3584,256]{2,1,0:T(8,128)(2,1)} %param.17) | copy-start | bytes 5505028
  77.7 28.2 %all-to-all-start.3 = ((bf16[8,448,256]{2,1,0:T(8,128)(2,1)}), bf16[8,448,256]{2,1,0:T(8,128)(2,1)}, u32[]{:S(2)}, u32[]{:S(2)}) async-start(bf16[8,448,256]{2,1,0:T(8,128)(2,1)} %bitcast.66), calls=%async_computation.3 | async-start | bytes 3670016 | tf_op jit(solution)/shard_map/all_to_all | solution.py:184
  82.1 60.3 %reduce-scatter.2.cloned.1.call-start = ((), (), s32[]{:S(2)}) async-start(), calls=%async_computation.13 | async-start | bytes 1474560 | tf_op jit(solution)/shard_map/reduce_scatter | solution.py:167
  105.9 41.8 %all-to-all-start.4 = ((bf16[8,448,256]{2,1,0:T(8,128)(2,1)}), bf16[8,448,256]{2,1,0:T(8,128)(2,1)}, u32[]{:S(2)}, u32[]{:S(2)}) async-start(bf16[8,448,256]{2,1,0:T(8,128)(2,1)} %bitcast.68), calls=%async_computation.4 | async-start | bytes 3670016 | tf_op jit(solution)/shard_map/all_to_all | solution.py:184
  110.2 64.8 %all-gather.5.cloned.1.call-start = ((), (), s32[]{:S(2)}) async-start(), calls=%async_computation.12 | async-start | bytes 1474560 | tf_op jit(solution)/shard_map/all_gather | solution.py:142
  111.7 4.1 %copy-start.12 = (bf16[576,3584]{1,0:T(8,128)(2,1)S(1)}, bf16[576,3584]{1,0:T(8,128)(2,1)}, u32[]{:S(2)}) copy-start(bf16[576,3584]{1,0:T(8,128)(2,1)} %all-gather.3.cloned.1.call-done) | copy-start | bytes 12386308
  111.7 4.5 %copy-start.13 = (bf16[1,3584,256]{2,1,0:T(8,128)(2,1)S(1)}, bf16[1,3584,256]{2,1,0:T(8,128)(2,1)}, u32[]{:S(2)}) copy-start(bf16[1,3584,256]{2,1,0:T(8,128)(2,1)} %param.18) | copy-start | bytes 5505028
  147.6 31.0 %all-to-all-start.6 = ((bf16[8,448,256]{2,1,0:T(8,128)(2,1)}), bf16[8,448,256]{2,1,0:T(8,128)(2,1)}, u32[]{:S(2)}, u32[]{:S(2)}) async-start(bf16[8,448,256]{2,1,0:T(8,128)(2,1)} %bitcast.69), calls=%async_computation.7 | async-start | bytes 3670016 | tf_op jit(solution)/shard_map/all_to_all | solution.py:184
  178.7 3.7 %copy-start.6 = (s32[8]{0:T(128)S(1)}, s32[8]{0:T(128)}, u32[]{:S(2)}) copy-start(s32[8]{0:T(128)} %placement_ref.1) | copy-start | bytes 100
  178.7 3.7 %copy-start.7 = (s32[8]{0:T(128)S(1)}, s32[8]{0:T(128)}, u32[]{:S(2)}) copy-start(s32[8]{0:T(128)} %plan_ref.1) | copy-start | bytes 100
  178.7 18.9 %all-to-all-start.1 = ((bf16[8,72,896]{2,1,0:T(8,128)(2,1)}), bf16[8,72,896]{2,1,0:T(8,128)(2,1)S(1)}, u32[]{:S(2)}, u32[]{:S(2)}) async-start(bf16[8,72,896]{2,1,0:T(8,128)(2,1)} %bitcast.70), calls=%async_computation.1 | async-start | bytes 2064384 | tf_op jit(solution)/shard_map/all_to_all | solution.py:147
  182.4 1.5 copy-start.1
  193.4 1.2 copy-start.2
  194.6 1.2 copy-start.3
  195.8 1.2 copy-start.5
  197.6 28.3 %copy-start.4 = (bf16[8,448,256]{2,1,0:T(8,128)(2,1)S(1)}, bf16[8,448,256]{2,1,0:T(8,128)(2,1)}, u32[]{:S(2)}) copy-start(bf16[8,448,256]{2,1,0:T(8,128)(2,1)} %copy-done.3) | copy-start | bytes 5505028
  252.8 28.2 %all-to-all-start.9 = ((bf16[8,448,256]{2,1,0:T(8,128)(2,1)}), bf16[8,448,256]{2,1,0:T(8,128)(2,1)}, u32[]{:S(2)}, u32[]{:S(2)}) async-start(bf16[8,448,256]{2,1,0:T(8,128)(2,1)} %copy-done.2), calls=%async_computation.10 | async-start | bytes 3670016 | tf_op jit(solution)/shard_map/all_to_all | solution.py:190
  280.9 3.0 %copy-start.8 = (bf16[8,448,256]{2,1,0:T(8,128)(2,1)S(1)}, bf16[8,448,256]{2,1,0:T(8,128)(2,1)}, u32[]{:S(2)}) copy-start(bf16[8,448,256]{2,1,0:T(8,128)(2,1)} %all_to_all.54) | copy-start | bytes 5505028
Sparse Core Ops, SparseCore 0:
  32.6 79.0 all-gather.2
  114.6 27.7 reduce-scatter.1
  144.5 30.4 all-gather.4

commit v2 on v1

--- a/solution.py
+++ b/solution.py
@@ -9,6 +9,7 @@
 
 D = 3584
 FF = 1024
+MESH = pl.DeviceIdType.MESH
 
 
 beta_first = 0.9
@@ -57,42 +58,131 @@
     )
 
 
-def update_kernel(
-    placement_ref, plan_ref, weight_ref, first_ref, second_ref, grad_ref, out_w, out_1, out_2
+def tail_kernel(
+    placement_ref, plan_ref, weight_ref, first_ref, second_ref, grad_ref,
+    out_w, out_1, out_2,
+    state, got, staged, load_sem, grad_send, grad_recv, out_send, out_recv,
 ):
-    held = placement_ref[plan_ref[pl.program_id(0)]]
-    slots, rows, _ = grad_ref.shape
+    slots, rows, columns = got.shape
+    me = lax.axis_index("expert")
+    outs = (out_w, out_1, out_2)
     chunk = math.gcd(rows, 112)
 
-    @pl.loop(0, rows // chunk)
-    def _(step):
-        part = pl.ds(pl.multiple_of(step * chunk, chunk), chunk)
-        gradient = jnp.zeros((chunk, grad_ref.shape[2]), jnp.float32)
-        for slot in range(slots):
-            share = jnp.where(placement_ref[slot] == held, 1.0, 0.0).astype(jnp.float32)
-            gradient = gradient + share * grad_ref[slot, part].astype(jnp.float32)
-        out_w[0, part], out_1[0, part], out_2[0, part] = adam_update(
-            gradient, weight_ref[0, part], first_ref[0, part], second_ref[0, part]
+    loads = [
+        pltpu.make_async_copy(ref, state.at[i], load_sem.at[i])
+        for i, ref in enumerate((weight_ref, first_ref, second_ref))
+    ]
+    for load in loads:
+        load.start()
+    own = pltpu.make_async_copy(grad_ref.at[me], got.at[me], load_sem.at[3])
+    own.start()
+
+    barrier = pltpu.get_barrier_semaphore()
+
+    @pl.loop(1, slots)
+    def _(k):
+        pl.semaphore_signal(
+            barrier, inc=1, device_id={"expert": lax.rem(me + k, slots)}, device_id_type=MESH
         )
+
+    pl.semaphore_wait(barrier, slots - 1)
+
+    def grad_copy(k):
+        peer = lax.rem(me + k, slots)
+        return pltpu.make_async_remote_copy(
+            src_ref=grad_ref.at[peer],
+            dst_ref=got.at[me],
+            send_sem=grad_send.at[k],
+            recv_sem=grad_recv.at[k],
+            device_id={"expert": peer},
+            device_id_type=MESH,
+        )
+
+    def out_copy(k, i):
+        return pltpu.make_async_remote_copy(
+            src_ref=staged.at[i, k],
+            dst_ref=outs[i].at[me],
+            send_sem=out_send.at[i, k],
+            recv_sem=out_recv.at[i, k],
+            device_id={"expert": lax.rem(me + k, slots)},
+            device_id_type=MESH,
+        )
+
+    @pl.loop(1, slots)
+    def _(k):
+        grad_copy(k).start()
+
+    for load in loads:
+        load.wait()
+    own.wait()
+
+    @pl.loop(1, slots)
+    def _(k):
+        grad_copy(k).wait()
+
+    def work_out(k):
+        old = plan_ref[lax.rem(me + k, slots)]
+        held = placement_ref[old]
+        shares = [
+            jnp.where(placement_ref[slot] == held, 1.0, 0.0).astype(jnp.float32)
+            for slot in range(slots)
+        ]
+
+        @pl.loop(0, rows // chunk)
+        def _(step):
+            part = pl.ds(pl.multiple_of(step * chunk, chunk), chunk)
+            gradient = jnp.zeros((chunk, columns), jnp.float32)
+            for slot in range(slots):
+                gradient = gradient + shares[slot] * got[slot, part].astype(jnp.float32)
+            staged[0, k, part], staged[1, k, part], staged[2, k, part] = adam_update(
+                gradient, state[0, old, part], state[1, old, part], state[2, old, part]
+            )
+
+    @pl.loop(1, slots)
+    def _(k):
+        work_out(k)
+        for i in range(3):
+            out_copy(k, i).start()
+
+    work_out(0)
+    kept = [
+        pltpu.make_async_copy(staged.at[i, 0], outs[i].at[me], load_sem.at[i]) for i in range(3)
+    ]
+    for copy in kept:
+        copy.start()
+    for copy in kept:
+        copy.wait()
+
+    @pl.loop(1, slots)
+    def _(k):
+        for i in range(3):
+            out_copy(k, i).wait()
 
 
 def update_slots(placement, plan, weight, first, second, grads):
     slots, rows, columns = weight.shape
-    taken = pl.BlockSpec((1, rows, columns), lambda s, held, plan: (plan[s], 0, 0))
-    every = pl.BlockSpec((slots, rows, columns), lambda s, held, plan: (0, 0, 0))
-    made = pl.BlockSpec((1, rows, columns), lambda s, held, plan: (s, 0, 0))
+    smem = pl.BlockSpec(memory_space=pltpu.SMEM)
+    anywhere = pl.BlockSpec(memory_space=pl.ANY)
     return pl.pallas_call(
-        update_kernel,
+        tail_kernel,
         out_shape=[jax.ShapeDtypeStruct(weight.shape, jnp.bfloat16)] * 3,
-        grid_spec=pltpu.PrefetchScalarGridSpec(
-            num_scalar_prefetch=2,
-            grid=(slots,),
-            in_specs=[taken, taken, taken, every],
-            out_specs=[made, made, made],
+        in_specs=[smem, smem, anywhere, anywhere, anywhere, anywhere],
+        out_specs=[anywhere] * 3,
+        scratch_shapes=[
+            pltpu.VMEM((3, slots, rows, columns), jnp.bfloat16),
+            pltpu.VMEM((slots, rows, columns), jnp.bfloat16),
+            pltpu.VMEM((3, slots, rows, columns), jnp.bfloat16),
+            pltpu.SemaphoreType.DMA((4,)),
+            pltpu.SemaphoreType.DMA((slots,)),
+            pltpu.SemaphoreType.DMA((slots,)),
+            pltpu.SemaphoreType.DMA((3, slots)),
+            pltpu.SemaphoreType.DMA((3, slots)),
+        ],
+        compiler_params=pltpu.CompilerParams(
+            collective_id=0, has_side_effects=True, vmem_limit_bytes=32 * 2**20
         ),
-        compiler_params=pltpu.CompilerParams(vmem_limit_bytes=32 * 2**20),
         cost_estimate=pl.CostEstimate(
-            flops=30 * weight.size, bytes_accessed=14 * weight.size, transcendentals=weight.size
+            flops=30 * weight.size, bytes_accessed=200 * weight.size, transcendentals=weight.size
         ),
     )(placement, plan, weight, first, second, grads)
 
@@ -135,7 +225,13 @@
         lax.all_to_all(sent_rows, "expert", split_axis=0, concat_axis=0, tiled=True),
         lax.all_to_all(sent_grads, "expert", split_axis=0, concat_axis=0, tiled=True),
     )
+    def exchange(array):
+        split = array.reshape(slot_count, array.shape[-2] // slot_count, array.shape[-1])
+        return lax.all_to_all(split, "expert", split_axis=0, concat_axis=0, tiled=True)
+
+    state_parts = [exchange(array[0]) for array in (gate_weight, first_moment, second_moment)]
     inputs = lax.all_gather(got_rows.reshape(buffer_size, quarter), "dp", axis=1, tiled=True)
+    inputs, *state_parts[:2] = lax.optimization_barrier((inputs, *state_parts[:2]))
     gate_values = jnp.dot(inputs, gate_weight[0], preferred_element_type=jnp.float32) * scale_in
     up_values = jnp.dot(inputs, up_weight[0], preferred_element_type=jnp.float32) * scale_in
     hidden = (jax.nn.silu(gate_values) * up_values).astype(jnp.bfloat16)
@@ -179,19 +275,9 @@
         )
         * scale_in
     )
-    def exchange(array):
-        split = array.reshape(slot_count, array.shape[-2] // slot_count, array.shape[-1])
-        return lax.all_to_all(split, "expert", split_axis=0, concat_axis=0, tiled=True)
-
-    state_parts = [exchange(array[0]) for array in (gate_weight, first_moment, second_moment)]
-    grad_parts = exchange(weight_grad.astype(jnp.bfloat16))
-    updated = update_slots(placement, migration_plan, *state_parts, grad_parts)
-    result = [
-        lax.all_to_all(array, "expert", split_axis=0, concat_axis=0, tiled=True).reshape(
-            first_moment.shape
-        )
-        for array in updated
-    ]
+    grad_blocks = weight_grad.astype(jnp.bfloat16).reshape(state_parts[0].shape)
+    updated = update_slots(placement, migration_plan, *state_parts, grad_blocks)
+    result = [array.reshape(first_moment.shape) for array in updated]
     return (layer_output, result[0], result[1], result[2])
 
 

time: 296 us -> 292 us (0.986)
  Pallas kernels: 9.45 us -> 86 us
  waiting for transfers between devices: 88.2 us -> 49.8 us
  blocking collectives: 120 us -> 94.1 us
  starting transfers between devices: 21.1 us -> 8.01 us
    pallas_call x1, Pallas kernels: 9.45 us -> 86 us  [update_slots(): pl.pallas_call(tail_kernel, out_shape=[jax.ShapeDtypeStruct(weight.shape,...]
    all_to_all x2 -> x0, blocking collectives: 55.2 us -> none  [per_device(): lax.all_to_all(array, 'expert', split_axis=0, concat_axis=0, tiled=True)]
    all_to_all x1 -> x2, blocking collectives: 26.9 us -> 55.2 us  [exchange(): lax.all_to_all(split, 'expert', split_axis=0, concat_axis=0, tiled=True)]
    all_gather x1, waiting for transfers between devices: 1.45 us -> 24 us  [per_device(): lax.all_gather(got_rows.reshape(buffer_size, quarter), 'dp', axis=1, tile...]
    all_gather x1, waiting for transfers between devices: 23 us -> 3.74 us  [per_device(): every_hidden = lax.all_gather(hidden, 'dp', axis=1, tiled=True)]
    reduce_scatter x1, waiting for transfers between devices: 24.1 us -> 6.15 us  [per_device(): lax.psum_scatter(partial_grad.astype(jnp.bfloat16), 'dp', scatter_dimensi...]
    all_to_all x1 -> x0, waiting for transfers between devices: 17.7 us -> none  [per_device(): lax.all_to_all(array, 'expert', split_axis=0, concat_axis=0, tiled=True)]
    all_to_all x3 -> x1, starting transfers between devices: 13 us -> 4.33 us  [exchange(): lax.all_to_all(split, 'expert', split_axis=0, concat_axis=0, tiled=True)]
  transfers between devices with their start and end apart: 8 -> 5, of which waited for: 6 -> 4; matrix products, arithmetic and copies ran while one was open for 8% -> 4% of each run, Pallas kernels for 3% -> 30%
where the time goes in v2:
time: 292 us; the launch traced here: 291 us
  blocking collectives  94.1 us (32%)
  Pallas kernels  86 us (29%)
  waiting for transfers between devices  49.8 us (17%)
  matrix products  18.8 us (6%)
  local copies, waits for them, and re-layouts  14.5 us (5%)
  between operations  13.9 us (5%)
  starting transfers between devices  8.01 us (3%)
  other arithmetic  5.68 us (2%)
    pallas_call x1, Pallas kernels, update_slots(): pl.pallas_call(tail_kernel, out_shape=[jax.ShapeDtypeStruct(weight.shape,...  86 us
    all_to_all x2, blocking collectives, exchange(): lax.all_to_all(split, 'expert', split_axis=0, concat_axis=0, tiled=True)  55.2 us
    all_gather x1, waiting for transfers between devices, per_device(): lax.all_gather(got_rows.reshape(buffer_size, quarter), 'dp', axis=1, tile...  24 us
    all_to_all x1, blocking collectives, per_device(): lax.all_to_all(sent_rows, 'expert', split_axis=0, concat_axis=0, tiled=True)  20.3 us
    all_to_all x1, blocking collectives, per_device(): lax.all_to_all(sent_grads, 'expert', split_axis=0, concat_axis=0, tiled=T...  18.6 us
    all_to_all x1, waiting for transfers between devices, exchange(): lax.all_to_all(split, 'expert', split_axis=0, concat_axis=0, tiled=True)  15.9 us
    unnamed x35, local copies, waits for them, and re-layouts  10.5 us
    reduce_scatter x1, waiting for transfers between devices, per_device(): lax.psum_scatter(partial_grad.astype(jnp.bfloat16), 'dp', scatter_dimensi...  6.15 us
  transfers between devices with their start and end apart: 5, of which 4 were waited for; matrix products, arithmetic and copies ran while one was open for 4% of the time, Pallas kernels for 30%

profile of v2, /device:TPU:0, one launch (start us, length us, event | category | flops | bytes accessed | tf_op | source)
XLA Modules:
  0.0 290.9 jit_solution(18325482174727666902)
XLA Ops:
  10.7 1.4 convolution_convert_fusion
  12.1 20.3 %all_to_all.30 = bf16[8,72,896]{2,1,0:T(8,128)(2,1)} all-to-all(bf16[8,72,896]{2,1,0:T(8,128)(2,1)S(1)} %bitcast.67), channel_id=1, replica_groups=mesh['dp'=4,'expert'=8] {'expert'}, dimensions={0} | all-to-all | bytes 2064384 | tf_op jit(solution)/shard_map/all_to_all | solution.py:225
  32.4 28.2 %all_to_all.31.weight_ref = bf16[8,448,256]{2,1,0:T(8,128)(2,1)} all-to-all(bf16[8,448,256]{2,1,0:T(8,128)(2,1)} %bitcast.69), channel_id=1, replica_groups=mesh['dp'=4,'expert'=8] {'expert'}, dimensions={0} | all-to-all | bytes 3670016 | tf_op jit(solution)/shard_map/all_to_all | solution.py:230
  60.7 26.9 %all_to_all.32.first_ref = bf16[8,448,256]{2,1,0:T(8,128)(2,1)} all-to-all(bf16[8,448,256]{2,1,0:T(8,128)(2,1)S(1)} %bitcast.68), channel_id=1, replica_groups=mesh['dp'=4,'expert'=8] {'expert'}, dimensions={0} | all-to-all | bytes 3670016 | tf_op jit(solution)/shard_map/all_to_all | solution.py:230
  87.6 24.0 %all-gather.3.cloned.1.call-done = bf16[576,3584]{1,0:T(8,128)(2,1)} async-done(((bf16[576,896]{1,0:T(8,128)(2,1)}), bf16[576,3584]{1,0:T(8,128)(2,1)}) %all-gather.3.cloned.1.call-update) | async-done | bytes 4128784 | tf_op jit(solution)/shard_map/all_gather | solution.py:233
  111.6 4.1 %fusion.14 = f32[576,256]{1,0:T(8,128)S(1)} fusion(bf16[576,3584]{1,0:T(8,128)(2,1)} %all-gather.3.cloned.1.call-done, bf16[1,3584,256]{2,1,0:T(8,128)(2,1)} %param.17), kind=kOutput, calls=%fused_computation.17 | convolution fusion | flops 1057112064 | bytes 6553600 | tf_op jit(solution)/shard_map/dot_general | solution.py:235
  116.1 2.1 multiply_convert_fusion.3
  119.0 18.6 %all_to_all.33 = bf16[8,72,896]{2,1,0:T(8,128)(2,1)S(1)} all-to-all(bf16[8,72,896]{2,1,0:T(8,128)(2,1)S(1)} %bitcast.66), channel_id=1, replica_groups=mesh['dp'=4,'expert'=8] {'expert'}, dimensions={0} | all-to-all | bytes 2064384 | tf_op jit(solution)/shard_map/all_to_all | solution.py:226
  137.6 2.4 fusion.9
  140.1 4.3 %all-to-all-start.4 = ((bf16[8,448,256]{2,1,0:T(8,128)(2,1)}), bf16[8,448,256]{2,1,0:T(8,128)(2,1)}, u32[]{:S(2)}, u32[]{:S(2)}) async-start(bf16[8,448,256]{2,1,0:T(8,128)(2,1)} %bitcast.70), calls=%async_computation.4 | async-start | bytes 3670016 | tf_op jit(solution)/shard_map/all_to_all | solution.py:230
  145.0 3.7 %all-gather.5.cloned.1.call-done = bf16[576,1024]{1,0:T(8,128)(2,1)} async-done(((bf16[576,256]{1,0:T(8,128)(2,1)}), bf16[576,1024]{1,0:T(8,128)(2,1)}) %all-gather.5.cloned.1.call-update) | async-done | bytes 1179664 | tf_op jit(solution)/shard_map/all_gather | solution.py:238
  148.7 3.6 %multiply_convert_fusion.1 = bf16[576,896]{1,0:T(8,128)(2,1)} fusion(bf16[576,1024]{1,0:T(8,128)(2,1)} %all-gather.5.cloned.1.call-done, bf16[1,1024,896]{2,1,0:T(8,128)(2,1)S(1)} %copy-done), kind=kOutput, calls=%fused_computation.6 | convolution fusion | flops 1057996800 | bytes 4046848 | tf_op jit(solution)/shard_map/dot_general | solution.py:241
  152.4 15.9 %all-to-all-done.4.second_ref = bf16[8,448,256]{2,1,0:T(8,128)(2,1)} async-done(((bf16[8,448,256]{2,1,0:T(8,128)(2,1)}), bf16[8,448,256]{2,1,0:T(8,128)(2,1)}, u32[]{:S(2)}, u32[]{:S(2)}) %all-to-all-start.4) | async-done | bytes 1835040 | tf_op jit(solution)/shard_map/all_to_all | solution.py:230
  168.3 3.6 %all-to-all-start.3 = ((bf16[8,72,896]{2,1,0:T(8,128)(2,1)}), bf16[8,72,896]{2,1,0:T(8,128)(2,1)S(1)}, u32[]{:S(2)}, u32[]{:S(2)}) async-start(bf16[8,72,896]{2,1,0:T(8,128)(2,1)} %bitcast.71), calls=%async_computation.3 | async-start | bytes 2064384 | tf_op jit(solution)/shard_map/all_to_all | solution.py:243
  173.0 6.2 %reduce-scatter.2.cloned.1.call-done = bf16[576,256]{1,0:T(8,128)(2,1)} async-done(((bf16[576,1024]{1,0:T(8,128)(2,1)}), bf16[576,256]{1,0:T(8,128)(2,1)}) %reduce-scatter.2.cloned.1.call-update) | async-done | bytes 294928 | tf_op jit(solution)/shard_map/reduce_scatter | solution.py:263
  179.2 4.5 %fusion = bf16[3584,256]{1,0:T(8,128)(2,1)S(1)} fusion(bf16[576,3584]{1,0:T(8,128)(2,1)} %all-gather.3.cloned.1.call-done, f32[576,256]{1,0:T(8,128)} %copy-done.15, f32[576,256]{1,0:T(8,128)} %get-tuple-element.31, bf16[576,256]{1,0:T(8,128)(2,1)} %reduce-scatter.2.cloned.1.call-done), kind=kOutput, calls=%fused_computation.4 | convolution fusion | flops 1060569088 | bytes 7438336 | tf_op jit(solution)/shard_map/dot_general | solution.py:273
  183.8 86.0 %shard_map.138 = (bf16[8,448,256]{2,1,0:T(8,128)(2,1)S(1)}, bf16[8,448,256]{2,1,0:T(8,128)(2,1)S(1)}, bf16[8,448,256]{2,1,0:T(8,128)(2,1)S(1)}) custom-call(s32[8]{0:T(128)S(1)} %copy-done.8, s32[8]{0:T(128)S(1)} %copy-done.9, bf16[8,448,256]{2,1,0:T(8,128)(2,1)S(1)} %copy-done.1, bf16[8,448,256]{2,1,0:T(8,128)(2,1)S(1)} %copy-done.2, ...), custom_call_target="tpu_custom_call" | custom-call | flops 27525120 | bytes 183500800 | tf_op jit(solution)/shard_map/pallas_call | solution.py:166
  269.8 1.3 copy-done.3
  271.1 1.2 copy-done.5
  272.3 1.2 copy-done.7
  276.3 1.6 add_convert_fusion
  277.9 3.0 %copy.27 = bf16[1,3584,256]{2,1,0:T(8,128)(2,1)} copy(bf16[1,3584,256]{2,1,0:T(8,128)(2,1)} %bitcast.60) | data formatting | bytes 3670016
  280.9 1.2 copy.28
  283.1 1.2 copy.29
  (57 shorter events, 10.2 us)
Async XLA Ops:
  7.2 130.5 %copy-start = (bf16[1,1024,896]{2,1,0:T(8,128)(2,1)S(1)}, bf16[1,1024,896]{2,1,0:T(8,128)(2,1)}, u32[]{:S(2)}) copy-start(bf16[1,1024,896]{2,1,0:T(8,128)(2,1)} %param.19) | copy-start | bytes 5505028
  7.2 104.4 %all-gather.3.cloned.1.call-start = ((), (), s32[]{:S(2)}) async-start(), calls=%async_computation.7 | async-start | bytes 5160960 | tf_op jit(solution)/shard_map/all_gather | solution.py:233
  32.4 116.4 %all-gather.5.cloned.1.call-start = ((), (), s32[]{:S(2)}) async-start(), calls=%async_computation.8 | async-start | bytes 1474560 | tf_op jit(solution)/shard_map/all_gather | solution.py:238
  32.4 28.3 %copy-start.10 = (bf16[1,3584,256]{2,1,0:T(8,128)(2,1)S(1)}, bf16[1,3584,256]{2,1,0:T(8,128)(2,1)}, u32[]{:S(2)}) copy-start(bf16[1,3584,256]{2,1,0:T(8,128)(2,1)} %param.20) | copy-start | bytes 5505028
  111.6 4.1 %copy-start.13 = (bf16[576,3584]{1,0:T(8,128)(2,1)S(1)}, bf16[576,3584]{1,0:T(8,128)(2,1)}, u32[]{:S(2)}) copy-start(bf16[576,3584]{1,0:T(8,128)(2,1)} %all-gather.3.cloned.1.call-done) | copy-start | bytes 12386308
  111.6 4.5 %copy-start.14 = (bf16[1,3584,256]{2,1,0:T(8,128)(2,1)S(1)}, bf16[1,3584,256]{2,1,0:T(8,128)(2,1)}, u32[]{:S(2)}) copy-start(bf16[1,3584,256]{2,1,0:T(8,128)(2,1)} %param.18) | copy-start | bytes 5505028
  116.1 2.1 copy-start.15
  116.1 2.2 copy-start.12
  116.1 2.4 copy-start.11
  118.3 60.9 %reduce-scatter.2.cloned.1.call-start = ((), (), s32[]{:S(2)}) async-start(), calls=%async_computation.9 | async-start | bytes 1474560 | tf_op jit(solution)/shard_map/reduce_scatter | solution.py:263
  140.1 28.2 %all-to-all-start.4 = ((bf16[8,448,256]{2,1,0:T(8,128)(2,1)}), bf16[8,448,256]{2,1,0:T(8,128)(2,1)}, u32[]{:S(2)}, u32[]{:S(2)}) async-start(bf16[8,448,256]{2,1,0:T(8,128)(2,1)} %bitcast.70), calls=%async_computation.4 | async-start | bytes 3670016 | tf_op jit(solution)/shard_map/all_to_all | solution.py:230
  168.3 105.3 %all-to-all-start.3 = ((bf16[8,72,896]{2,1,0:T(8,128)(2,1)}), bf16[8,72,896]{2,1,0:T(8,128)(2,1)S(1)}, u32[]{:S(2)}, u32[]{:S(2)}) async-start(bf16[8,72,896]{2,1,0:T(8,128)(2,1)} %bitcast.71), calls=%async_computation.3 | async-start | bytes 2064384 | tf_op jit(solution)/shard_map/all_to_all | solution.py:243
  179.2 4.6 %copy-start.1 = (bf16[8,448,256]{2,1,0:T(8,128)(2,1)S(1)}, bf16[8,448,256]{2,1,0:T(8,128)(2,1)}, u32[]{:S(2)}) copy-start(bf16[8,448,256]{2,1,0:T(8,128)(2,1)} %all_to_all.31.weight_ref) | copy-start | bytes 5505028
  179.2 4.6 %copy-start.2 = (bf16[8,448,256]{2,1,0:T(8,128)(2,1)S(1)}, bf16[8,448,256]{2,1,0:T(8,128)(2,1)}, u32[]{:S(2)}) copy-start(bf16[8,448,256]{2,1,0:T(8,128)(2,1)} %all_to_all.32.first_ref) | copy-start | bytes 5505028
  179.2 4.6 %copy-start.8 = (s32[8]{0:T(128)S(1)}, s32[8]{0:T(128)}, u32[]{:S(2)}) copy-start(s32[8]{0:T(128)} %placement_ref.1) | copy-start | bytes 100
  179.2 4.6 %copy-start.9 = (s32[8]{0:T(128)S(1)}, s32[8]{0:T(128)}, u32[]{:S(2)}) copy-start(s32[8]{0:T(128)} %plan_ref.1) | copy-start | bytes 100
  269.8 1.3 copy-start.3
  271.1 1.2 copy-start.5
  272.3 1.2 copy-start.7
  277.9 3.0 %copy-start.6 = (bf16[8,448,256]{2,1,0:T(8,128)(2,1)S(1)}, bf16[8,448,256]{2,1,0:T(8,128)(2,1)}, u32[]{:S(2)}) copy-start(bf16[8,448,256]{2,1,0:T(8,128)(2,1)} %copy-done.5) | copy-start | bytes 5505028
  280.9 2.2 copy-start.4
Sparse Core Ops, SparseCore 0:
  32.5 79.0 all-gather.2
  118.4 30.3 all-gather.4
  151.6 27.4 reduce-scatter.1

commit v3 on v2

--- a/solution.py
+++ b/solution.py
@@ -216,26 +216,36 @@
     landing = target[None, :, :] == buffer_slots[:, None, None]
     selection = jnp.any(landing, -1).astype(jnp.bfloat16)
     row_weight = jnp.sum(jnp.where(landing, route_weight[None], jnp.float32(0.0)), (1, 2))
-    sent_rows = jnp.dot(selection, tokens, preferred_element_type=jnp.float32).astype(jnp.bfloat16)
+    cut = quarter // 256 * 128
+    kept = quarter - cut
+    late = jnp.dot(selection, tokens[:, :kept], preferred_element_type=jnp.float32)
+    wide = lax.all_gather(tokens[:, kept:], "dp", axis=1, tiled=True)
+    early = jnp.dot(selection, wide, preferred_element_type=jnp.float32).astype(jnp.bfloat16)
     picked_grads = jnp.dot(selection, cotangent, preferred_element_type=jnp.float32)
     sent_grads = (row_weight[:, None] * picked_grads).astype(jnp.bfloat16)
-    sent_rows = sent_rows.reshape(slot_count, capacity, quarter)
-    sent_grads = sent_grads.reshape(slot_count, capacity, quarter)
-    got_rows, got_grads = (
-        lax.all_to_all(sent_rows, "expert", split_axis=0, concat_axis=0, tiled=True),
-        lax.all_to_all(sent_grads, "expert", split_axis=0, concat_axis=0, tiled=True),
-    )
-    def exchange(array):
-        split = array.reshape(slot_count, array.shape[-2] // slot_count, array.shape[-1])
-        return lax.all_to_all(split, "expert", split_axis=0, concat_axis=0, tiled=True)
-
-    state_parts = [exchange(array[0]) for array in (gate_weight, first_moment, second_moment)]
-    inputs = lax.all_gather(got_rows.reshape(buffer_size, quarter), "dp", axis=1, tiled=True)
-    inputs, *state_parts[:2] = lax.optimization_barrier((inputs, *state_parts[:2]))
+
+    def trade(rows):
+        blocks = rows.reshape(slot_count, rows.shape[0] // slot_count, rows.shape[1])
+        return lax.all_to_all(blocks, "expert", split_axis=0, concat_axis=0, tiled=True)
+
+    got_late = trade(late.astype(jnp.bfloat16)).reshape(buffer_size, kept)
+    got_late, sent_grads = lax.optimization_barrier((got_late, sent_grads))
+    late = lax.all_gather(got_late, "dp", axis=1, tiled=True)
+    got_grads = trade(sent_grads)
+    got_grads, early = lax.optimization_barrier((got_grads, early))
+    early = trade(early).reshape(buffer_size, wide.shape[1])
+    early, *states = lax.optimization_barrier((early, gate_weight, first_moment, second_moment))
+    state_parts = [trade(array[0]) for array in states]
+    pieces = []
+    for part in range(lax.axis_size("dp")):
+        pieces.append(late[:, part * kept : (part + 1) * kept])
+        pieces.append(early[:, part * cut : (part + 1) * cut])
+    inputs = jnp.concatenate(pieces, axis=1)
     gate_values = jnp.dot(inputs, gate_weight[0], preferred_element_type=jnp.float32) * scale_in
     up_values = jnp.dot(inputs, up_weight[0], preferred_element_type=jnp.float32) * scale_in
     hidden = (jax.nn.silu(gate_values) * up_values).astype(jnp.bfloat16)
     every_hidden = lax.all_gather(hidden, "dp", axis=1, tiled=True)
+    every_hidden, *state_parts = lax.optimization_barrier((every_hidden, *state_parts))
     w_down = down_weight[0]
     outputs = (
         jnp.dot(every_hidden, w_down, preferred_element_type=jnp.float32) * scale_mid

time: 292 us -> 292 us (level)
  blocking collectives: 94.1 us -> 47.5 us
  starting transfers between devices: 8.01 us -> 25.4 us
  waiting for transfers between devices: 49.8 us -> 65.5 us
  local copies, waits for them, and re-layouts: 14.5 us -> 23.4 us
  Pallas kernels: 86 us -> 90.1 us
    all_to_all x4 -> x1, blocking collectives: 94.1 us -> 27.4 us  [trade(): lax.all_to_all(blocks, 'expert', split_axis=0, concat_axis=0, tiled=True)]
    all_to_all x1 -> x5, waiting for transfers between devices: 15.9 us -> 65.4 us  [trade(): lax.all_to_all(blocks, 'expert', split_axis=0, concat_axis=0, tiled=True)]
    all_gather x1, waiting for transfers between devices: 24 us -> 0.02 us  [per_device(): late = lax.all_gather(got_late, 'dp', axis=1, tiled=True)]
    all_gather x0 -> x1, blocking collectives: none -> 20.1 us  [per_device(): wide = lax.all_gather(tokens[:, kept:], 'dp', axis=1, tiled=True)]
    all_to_all x1 -> x5, starting transfers between devices: 4.33 us -> 21.7 us  [trade(): lax.all_to_all(blocks, 'expert', split_axis=0, concat_axis=0, tiled=True)]
    unnamed x35 -> x42, local copies, waits for them, and re-layouts: 10.5 us -> 18.5 us
    reduce_scatter x1, waiting for transfers between devices: 6.15 us -> 0.01 us  [per_device(): lax.psum_scatter(partial_grad.astype(jnp.bfloat16), 'dp', scatter_dimensi...]
    pallas_call x1, Pallas kernels: 86 us -> 90.1 us  [update_slots(): pl.pallas_call(tail_kernel, out_shape=[jax.ShapeDtypeStruct(weight.shape,...]
  transfers between devices with their start and end apart: 5 -> 9, of which waited for: 4 -> 4; matrix products, arithmetic and copies ran while one was open for 4% -> 9% of each run, Pallas kernels for 30% -> 31%
where the time goes in v3:
time: 292 us; the launch traced here: 291 us
  Pallas kernels  90.1 us (31%)
  waiting for transfers between devices  65.5 us (22%)
  blocking collectives  47.5 us (16%)
  starting transfers between devices  25.4 us (9%)
  local copies, waits for them, and re-layouts  23.4 us (8%)
  matrix products  19.3 us (7%)
  between operations  14 us (5%)
  other arithmetic  5.74 us (2%)
    pallas_call x1, Pallas kernels, update_slots(): pl.pallas_call(tail_kernel, out_shape=[jax.ShapeDtypeStruct(weight.shape,...  90.1 us
    all_to_all x5, waiting for transfers between devices, trade(): lax.all_to_all(blocks, 'expert', split_axis=0, concat_axis=0, tiled=True)  65.4 us
    all_to_all x1, blocking collectives, trade(): lax.all_to_all(blocks, 'expert', split_axis=0, concat_axis=0, tiled=True)  27.4 us
    all_to_all x5, starting transfers between devices, trade(): lax.all_to_all(blocks, 'expert', split_axis=0, concat_axis=0, tiled=True)  21.7 us
    all_gather x1, blocking collectives, per_device(): wide = lax.all_gather(tokens[:, kept:], 'dp', axis=1, tiled=True)  20.1 us
    unnamed x42, local copies, waits for them, and re-layouts  18.5 us
  transfers between devices with their start and end apart: 9, of which 4 were waited for; matrix products, arithmetic and copies ran while one was open for 9% of the time, Pallas kernels for 31%

profile of v3, /device:TPU:0, one launch (start us, length us, event | category | flops | bytes accessed | tf_op | source)
XLA Modules:
  0.0 290.9 jit_solution(5162780598641229511)
XLA Ops:
  10.7 2.0 convolution_convert_fusion.1
  12.7 5.2 %all-to-all-start = ((bf16[8,72,512]{2,1,0:T(8,128)(2,1)}), bf16[8,72,512]{2,1,0:T(8,128)(2,1)S(1)}, u32[]{:S(2)}, u32[]{:S(2)}) async-start(bf16[8,72,512]{2,1,0:T(8,128)(2,1)} %bitcast.2), calls=%async_computation | async-start | bytes 1179648 | tf_op jit(solution)/shard_map/all_to_all | solution.py:229
  18.2 1.4 multiply_convert_fusion.1
  19.6 8.8 %all-to-all-done = bf16[8,72,512]{2,1,0:T(8,128)(2,1)S(1)} async-done(((bf16[8,72,512]{2,1,0:T(8,128)(2,1)}), bf16[8,72,512]{2,1,0:T(8,128)(2,1)S(1)}, u32[]{:S(2)}, u32[]{:S(2)}) %all-to-all-start) | async-done | bytes 589856 | tf_op jit(solution)/shard_map/all_to_all | solution.py:229
  29.2 3.6 %all-to-all-start.1 = ((bf16[8,72,896]{2,1,0:T(8,128)(2,1)}), bf16[8,72,896]{2,1,0:T(8,128)(2,1)S(1)}, u32[]{:S(2)}, u32[]{:S(2)}) async-start(bf16[8,72,896]{2,1,0:T(8,128)(2,1)} %bitcast.4), calls=%async_computation.1 | async-start | bytes 2064384 | tf_op jit(solution)/shard_map/all_to_all | solution.py:229
  33.7 20.1 %all_gather.10 = bf16[128,1536]{1,0:T(8,128)(2,1)S(1)} all-gather(bf16[128,384]{1,0:T(8,128)(2,1)S(1)} %slice.51), channel_id=1, replica_groups=mesh['dp'=4,'expert'=8] {'dp'}, dimensions={1}, use_global_device_ids=true | all-gather | bytes 491520 | tf_op jit(solution)/shard_map/all_gather | solution.py:222
  53.8 1.8 convolution_convert_fusion
  55.6 27.4 %all_to_all.35 = bf16[8,72,1536]{2,1,0:T(8,128)(2,1)} all-to-all(bf16[8,72,1536]{2,1,0:T(8,128)(2,1)} %bitcast.72), channel_id=1, replica_groups=mesh['dp'=4,'expert'=8] {'expert'}, dimensions={0} | all-to-all | bytes 3538944 | tf_op jit(solution)/shard_map/all_to_all | solution.py:229
  83.0 4.3 %all-to-all-start.3 = ((bf16[8,448,256]{2,1,0:T(8,128)(2,1)}), bf16[8,448,256]{2,1,0:T(8,128)(2,1)}, u32[]{:S(2)}, u32[]{:S(2)}) async-start(bf16[8,448,256]{2,1,0:T(8,128)(2,1)} %bitcast.74), calls=%async_computation.3 | async-start | bytes 3670016 | tf_op jit(solution)/shard_map/all_to_all | solution.py:229
  90.9 1.2 slice_dynamic-update-slice_fusion.1
  96.3 2.1 multiply_convert_fusion.3
  98.5 12.7 %all-to-all-done.3.weight_ref = bf16[8,448,256]{2,1,0:T(8,128)(2,1)} async-done(((bf16[8,448,256]{2,1,0:T(8,128)(2,1)}), bf16[8,448,256]{2,1,0:T(8,128)(2,1)}, u32[]{:S(2)}, u32[]{:S(2)}) %all-to-all-start.3) | async-done | bytes 1835040 | tf_op jit(solution)/shard_map/all_to_all | solution.py:229
  111.1 4.3 %all-to-all-start.4 = ((bf16[8,448,256]{2,1,0:T(8,128)(2,1)}), bf16[8,448,256]{2,1,0:T(8,128)(2,1)}, u32[]{:S(2)}, u32[]{:S(2)}) async-start(bf16[8,448,256]{2,1,0:T(8,128)(2,1)} %bitcast.75), calls=%async_computation.4 | async-start | bytes 3670016 | tf_op jit(solution)/shard_map/all_to_all | solution.py:229
  115.5 2.4 fusion.9
  118.0 21.3 %all-to-all-done.4.first_ref = bf16[8,448,256]{2,1,0:T(8,128)(2,1)} async-done(((bf16[8,448,256]{2,1,0:T(8,128)(2,1)}), bf16[8,448,256]{2,1,0:T(8,128)(2,1)}, u32[]{:S(2)}, u32[]{:S(2)}) %all-to-all-start.4) | async-done | bytes 1835040 | tf_op jit(solution)/shard_map/all_to_all | solution.py:229
  139.3 4.3 %all-to-all-start.5 = ((bf16[8,448,256]{2,1,0:T(8,128)(2,1)}), bf16[8,448,256]{2,1,0:T(8,128)(2,1)}, u32[]{:S(2)}, u32[]{:S(2)}) async-start(bf16[8,448,256]{2,1,0:T(8,128)(2,1)} %bitcast.76), calls=%async_computation.5 | async-start | bytes 3670016 | tf_op jit(solution)/shard_map/all_to_all | solution.py:229
  144.9 22.6 %all-to-all-done.5.second_ref = bf16[8,448,256]{2,1,0:T(8,128)(2,1)} async-done(((bf16[8,448,256]{2,1,0:T(8,128)(2,1)}), bf16[8,448,256]{2,1,0:T(8,128)(2,1)}, u32[]{:S(2)}, u32[]{:S(2)}) %all-to-all-start.5) | async-done | bytes 1835040 | tf_op jit(solution)/shard_map/all_to_all | solution.py:229
  167.5 3.6 %multiply_convert_fusion = bf16[576,896]{1,0:T(8,128)(2,1)} fusion(bf16[576,1024]{1,0:T(8,128)(2,1)} %all-gather.5.cloned.1.call-done, bf16[1,1024,896]{2,1,0:T(8,128)(2,1)S(1)} %copy-done), kind=kOutput, calls=%fused_computation.6 | convolution fusion | flops 1057996800 | bytes 4046848 | tf_op jit(solution)/shard_map/dot_general | solution.py:251
  171.1 3.6 %all-to-all-start.6 = ((bf16[8,72,896]{2,1,0:T(8,128)(2,1)}), bf16[8,72,896]{2,1,0:T(8,128)(2,1)S(1)}, u32[]{:S(2)}, u32[]{:S(2)}) async-start(bf16[8,72,896]{2,1,0:T(8,128)(2,1)} %bitcast.78), calls=%async_computation.6 | async-start | bytes 2064384 | tf_op jit(solution)/shard_map/all_to_all | solution.py:253
  175.3 4.4 %fusion = bf16[3584,256]{1,0:T(8,128)(2,1)S(1)} fusion(bf16[576,3584]{1,0:T(8,128)(2,1)} %copy-done.12, f32[576,256]{1,0:T(8,128)} %copy-done.15, f32[576,256]{1,0:T(8,128)} %get-tuple-element.49, bf16[576,256]{1,0:T(8,128)(2,1)} %reduce-scatter.2.cloned.1.call-done), kind=kOutput, calls=%fused_computation.4 | convolution fusion | flops 1060569088 | bytes 7438336 | tf_op jit(solution)/shard_map/dot_general | solution.py:283
  179.8 90.1 %shard_map.138 = (bf16[8,448,256]{2,1,0:T(8,128)(2,1)S(1)}, bf16[8,448,256]{2,1,0:T(8,128)(2,1)S(1)}, bf16[8,448,256]{2,1,0:T(8,128)(2,1)S(1)}) custom-call(s32[8]{0:T(128)S(1)} %copy-done.6, s32[8]{0:T(128)S(1)} %copy-done.7, bf16[8,448,256]{2,1,0:T(8,128)(2,1)} %all-to-all-done.3.weight_ref, bf16[8,448,256]{2,1,0:T(8,128)(2,1)} %all-to-all-done.4.first_ref, ...), custom_call_target="tpu_custom_call" | custom-call | flops 27525120 | bytes 183500800 | tf_op jit(solution)/shard_map/pallas_call | solution.py:166
  269.8 1.3 copy-done.1
  276.3 1.6 add_convert_fusion
  278.0 3.0 %copy.34 = bf16[1,3584,256]{2,1,0:T(8,128)(2,1)} copy(bf16[1,3584,256]{2,1,0:T(8,128)(2,1)} %bitcast.63) | data formatting | bytes 3670016
  (73 shorter events, 23.6 us)
Async XLA Ops:
  7.2 108.4 %copy-start = (bf16[1,1024,896]{2,1,0:T(8,128)(2,1)S(1)}, bf16[1,1024,896]{2,1,0:T(8,128)(2,1)}, u32[]{:S(2)}) copy-start(bf16[1,1024,896]{2,1,0:T(8,128)(2,1)} %param.19) | copy-start | bytes 5505028
  7.2 10.8 %copy-start.13 = (f32[128,3]{0,1:T(4,128)S(1)}, f32[128,3]{0,1:T(4,128)}, u32[]{:S(2)}) copy-start(f32[128,3]{0,1:T(4,128)} %param.16) | copy-start | bytes 4612
  7.2 11.0 %copy-start.11 = (bf16[128,896]{1,0:T(8,128)(2,1)S(1)}, bf16[128,896]{1,0:T(8,128)(2,1)}, u32[]{:S(2)}) copy-start(bf16[128,896]{1,0:T(8,128)(2,1)} %param.14) | copy-start | bytes 688132
  12.7 15.6 %all-to-all-start = ((bf16[8,72,512]{2,1,0:T(8,128)(2,1)}), bf16[8,72,512]{2,1,0:T(8,128)(2,1)S(1)}, u32[]{:S(2)}, u32[]{:S(2)}) async-start(bf16[8,72,512]{2,1,0:T(8,128)(2,1)} %bitcast.2), calls=%async_computation | async-start | bytes 1179648 | tf_op jit(solution)/shard_map/all_to_all | solution.py:229
  17.9 69.5 %all-gather.3.cloned.1.call-start = ((), (), s32[]{:S(2)}) async-start(), calls=%async_computation.8 | async-start | bytes 2949120 | tf_op jit(solution)/shard_map/all_gather | solution.py:233
  29.2 26.4 %all-to-all-start.1 = ((bf16[8,72,896]{2,1,0:T(8,128)(2,1)}), bf16[8,72,896]{2,1,0:T(8,128)(2,1)S(1)}, u32[]{:S(2)}, u32[]{:S(2)}) async-start(bf16[8,72,896]{2,1,0:T(8,128)(2,1)} %bitcast.4), calls=%async_computation.1 | async-start | bytes 2064384 | tf_op jit(solution)/shard_map/all_to_all | solution.py:229
  83.0 28.2 %all-to-all-start.3 = ((bf16[8,448,256]{2,1,0:T(8,128)(2,1)}), bf16[8,448,256]{2,1,0:T(8,128)(2,1)}, u32[]{:S(2)}, u32[]{:S(2)}) async-start(bf16[8,448,256]{2,1,0:T(8,128)(2,1)} %bitcast.74), calls=%async_computation.3 | async-start | bytes 3670016 | tf_op jit(solution)/shard_map/all_to_all | solution.py:229
  87.3 80.2 %all-gather.5.cloned.1.call-start = ((), (), s32[]{:S(2)}) async-start(), calls=%async_computation.9 | async-start | bytes 1474560 | tf_op jit(solution)/shard_map/all_gather | solution.py:247
  87.4 3.4 %copy-start.8 = (bf16[8,72,1536]{2,1,0:T(8,128)(2,1)S(1)}, bf16[8,72,1536]{2,1,0:T(8,128)(2,1)}, u32[]{:S(2)}) copy-start(bf16[8,72,1536]{2,1,0:T(8,128)(2,1)} %all_to_all.35) | copy-start | bytes 5308420
  90.9 2.5 copy-start.10
  93.4 2.0 copy-start.12
  93.4 2.9 copy-start.14
  96.3 2.1 copy-start.15
  111.1 28.2 %all-to-all-start.4 = ((bf16[8,448,256]{2,1,0:T(8,128)(2,1)}), bf16[8,448,256]{2,1,0:T(8,128)(2,1)}, u32[]{:S(2)}, u32[]{:S(2)}) async-start(bf16[8,448,256]{2,1,0:T(8,128)(2,1)} %bitcast.75), calls=%async_computation.4 | async-start | bytes 3670016 | tf_op jit(solution)/shard_map/all_to_all | solution.py:229
  115.5 59.8 %reduce-scatter.2.cloned.1.call-start = ((), (), s32[]{:S(2)}) async-start(), calls=%async_computation.10 | async-start | bytes 1474560 | tf_op jit(solution)/shard_map/reduce_scatter | solution.py:273
  139.3 28.2 %all-to-all-start.5 = ((bf16[8,448,256]{2,1,0:T(8,128)(2,1)}), bf16[8,448,256]{2,1,0:T(8,128)(2,1)}, u32[]{:S(2)}, u32[]{:S(2)}) async-start(bf16[8,448,256]{2,1,0:T(8,128)(2,1)} %bitcast.76), calls=%async_computation.5 | async-start | bytes 3670016 | tf_op jit(solution)/shard_map/all_to_all | solution.py:229
  171.1 102.4 %all-to-all-start.6 = ((bf16[8,72,896]{2,1,0:T(8,128)(2,1)}), bf16[8,72,896]{2,1,0:T(8,128)(2,1)S(1)}, u32[]{:S(2)}, u32[]{:S(2)}) async-start(bf16[8,72,896]{2,1,0:T(8,128)(2,1)} %bitcast.78), calls=%async_computation.6 | async-start | bytes 2064384 | tf_op jit(solution)/shard_map/all_to_all | solution.py:253
  175.3 4.4 %copy-start.6 = (s32[8]{0:T(128)S(1)}, s32[8]{0:T(128)}, u32[]{:S(2)}) copy-start(s32[8]{0:T(128)} %placement_ref.1) | copy-start | bytes 100
  175.3 4.4 %copy-start.7 = (s32[8]{0:T(128)S(1)}, s32[8]{0:T(128)}, u32[]{:S(2)}) copy-start(s32[8]{0:T(128)} %plan_ref.1) | copy-start | bytes 100
  269.8 1.3 copy-start.1
  271.1 1.2 copy-start.3
  272.3 1.2 copy-start.5
  278.0 3.0 %copy-start.4 = (bf16[8,448,256]{2,1,0:T(8,128)(2,1)S(1)}, bf16[8,448,256]{2,1,0:T(8,128)(2,1)}, u32[]{:S(2)}) copy-start(bf16[8,448,256]{2,1,0:T(8,128)(2,1)} %copy-done.3) | copy-start | bytes 5505028
  280.9 2.2 copy-start.2
  (1 other events, 0.8 us)
Sparse Core Ops, SparseCore 0:
  29.3 54.9 all-gather.2
  98.6 31.8 all-gather.4
  133.4 27.4 reduce-scatter.1

commit v4 on v3

--- a/solution.py
+++ b/solution.py
@@ -216,7 +216,7 @@
     landing = target[None, :, :] == buffer_slots[:, None, None]
     selection = jnp.any(landing, -1).astype(jnp.bfloat16)
     row_weight = jnp.sum(jnp.where(landing, route_weight[None], jnp.float32(0.0)), (1, 2))
-    cut = quarter // 256 * 128
+    cut = quarter // 384 * 128
     kept = quarter - cut
     late = jnp.dot(selection, tokens[:, :kept], preferred_element_type=jnp.float32)
     wide = lax.all_gather(tokens[:, kept:], "dp", axis=1, tiled=True)

time: 292 us -> 284 us (0.973)
  blocking collectives: 47.5 us -> 37.4 us
  waiting for transfers between devices: 65.5 us -> 69.1 us
    all_gather x1, waiting for transfers between devices: 0.02 us -> 15.8 us  [per_device(): late = lax.all_gather(got_late, 'dp', axis=1, tiled=True)]
    all_to_all x5, waiting for transfers between devices: 65.4 us -> 53.2 us  [trade(): lax.all_to_all(blocks, 'expert', split_axis=0, concat_axis=0, tiled=True)]
    all_to_all x1, blocking collectives: 27.4 us -> 20.7 us  [trade(): lax.all_to_all(blocks, 'expert', split_axis=0, concat_axis=0, tiled=True)]
    all_gather x1, blocking collectives: 20.1 us -> 16.7 us  [per_device(): wide = lax.all_gather(tokens[:, kept:], 'dp', axis=1, tiled=True)]
    unnamed x42 -> x44, local copies, waits for them, and re-layouts: 18.5 us -> 16.7 us
  transfers between devices with their start and end apart: 9 -> 9, of which waited for: 4 -> 4; matrix products, arithmetic and copies ran while one was open for 9% -> 8% of each run, Pallas kernels for 31% -> 32%
where the time goes in v4:
time: 284 us; the launch traced here: 282 us
  Pallas kernels  90.1 us (32%)
  waiting for transfers between devices  69.1 us (24%)
  blocking collectives  37.4 us (13%)
  starting transfers between devices  26.3 us (9%)
  local copies, waits for them, and re-layouts  20.6 us (7%)
  matrix products  19.2 us (7%)
  between operations  14.1 us (5%)
  other arithmetic  5.67 us (2%)
    pallas_call x1, Pallas kernels, update_slots(): pl.pallas_call(tail_kernel, out_shape=[jax.ShapeDtypeStruct(weight.shape,...  90.1 us
    all_to_all x5, waiting for transfers between devices, trade(): lax.all_to_all(blocks, 'expert', split_axis=0, concat_axis=0, tiled=True)  53.2 us
    all_to_all x5, starting transfers between devices, trade(): lax.all_to_all(blocks, 'expert', split_axis=0, concat_axis=0, tiled=True)  22.6 us
    all_to_all x1, blocking collectives, trade(): lax.all_to_all(blocks, 'expert', split_axis=0, concat_axis=0, tiled=True)  20.7 us
    all_gather x1, blocking collectives, per_device(): wide = lax.all_gather(tokens[:, kept:], 'dp', axis=1, tiled=True)  16.7 us
    unnamed x44, local copies, waits for them, and re-layouts  16.7 us
    all_gather x1, waiting for transfers between devices, per_device(): late = lax.all_gather(got_late, 'dp', axis=1, tiled=True)  15.8 us
  transfers between devices with their start and end apart: 9, of which 4 were waited for; matrix products, arithmetic and copies ran while one was open for 8% of the time, Pallas kernels for 32%

profile of v4, /device:TPU:0, one launch (start us, length us, event | category | flops | bytes accessed | tf_op | source)
XLA Modules:
  0.0 282.5 jit_solution(9694680571424288429)
XLA Ops:
  10.7 2.1 convolution_convert_fusion.1
  12.8 5.2 %all-to-all-start = ((bf16[8,72,640]{2,1,0:T(8,128)(2,1)}), bf16[8,72,640]{2,1,0:T(8,128)(2,1)S(1)}, u32[]{:S(2)}, u32[]{:S(2)}) async-start(bf16[8,72,640]{2,1,0:T(8,128)(2,1)} %bitcast.2), calls=%async_computation | async-start | bytes 1474560 | tf_op jit(solution)/shard_map/all_to_all | solution.py:229
  18.3 1.4 multiply_convert_fusion.1
  19.7 10.4 %all-to-all-done = bf16[8,72,640]{2,1,0:T(8,128)(2,1)S(1)} async-done(((bf16[8,72,640]{2,1,0:T(8,128)(2,1)}), bf16[8,72,640]{2,1,0:T(8,128)(2,1)S(1)}, u32[]{:S(2)}, u32[]{:S(2)}) %all-to-all-start) | async-done | bytes 737312 | tf_op jit(solution)/shard_map/all_to_all | solution.py:229
  31.0 4.3 %all-to-all-start.1 = ((bf16[8,72,896]{2,1,0:T(8,128)(2,1)}), bf16[8,72,896]{2,1,0:T(8,128)(2,1)}, u32[]{:S(2)}, u32[]{:S(2)}) async-start(bf16[8,72,896]{2,1,0:T(8,128)(2,1)} %bitcast.4), calls=%async_computation.1 | async-start | bytes 2064384 | tf_op jit(solution)/shard_map/all_to_all | solution.py:229
  35.3 16.7 %all_gather.10 = bf16[128,1024]{1,0:T(8,128)(2,1)S(1)} all-gather(bf16[128,256]{1,0:T(8,128)(2,1)S(1)} %slice-done), channel_id=1, replica_groups=mesh['dp'=4,'expert'=8] {'dp'}, dimensions={1}, use_global_device_ids=true | all-gather | bytes 327680 | tf_op jit(solution)/shard_map/all_gather | solution.py:222
  52.4 20.7 %all_to_all.35 = bf16[8,72,1024]{2,1,0:T(8,128)(2,1)} all-to-all(bf16[8,72,1024]{2,1,0:T(8,128)(2,1)S(1)} %bitcast.68), channel_id=1, replica_groups=mesh['dp'=4,'expert'=8] {'expert'}, dimensions={0} | all-to-all | bytes 2359296 | tf_op jit(solution)/shard_map/all_to_all | solution.py:229
  73.1 4.5 %all-to-all-start.3 = ((bf16[8,448,256]{2,1,0:T(8,128)(2,1)}), bf16[8,448,256]{2,1,0:T(8,128)(2,1)}, u32[]{:S(2)}, u32[]{:S(2)}) async-start(bf16[8,448,256]{2,1,0:T(8,128)(2,1)} %bitcast.74), calls=%async_computation.3 | async-start | bytes 3670016 | tf_op jit(solution)/shard_map/all_to_all | solution.py:229
  77.7 15.8 %all-gather.3.cloned.1.call-done = bf16[576,2560]{1,0:T(8,128)(2,1)} async-done(((bf16[576,640]{1,0:T(8,128)(2,1)}), bf16[576,2560]{1,0:T(8,128)(2,1)}) %all-gather.3.cloned.1.call-update) | async-done | bytes 2949136 | tf_op jit(solution)/shard_map/all_gather | solution.py:233
  93.5 1.3 slice_dynamic-update-slice_fusion.3
  100.5 2.1 multiply_convert_fusion.3
  102.7 4.3 %all-to-all-start.4 = ((bf16[8,448,256]{2,1,0:T(8,128)(2,1)}), bf16[8,448,256]{2,1,0:T(8,128)(2,1)}, u32[]{:S(2)}, u32[]{:S(2)}) async-start(bf16[8,448,256]{2,1,0:T(8,128)(2,1)} %bitcast.75), calls=%async_computation.4 | async-start | bytes 3670016 | tf_op jit(solution)/shard_map/all_to_all | solution.py:229
  107.1 3.6 %fusion.9 = bf16[576,1024]{1,0:T(8,128)(2,1)} fusion(bf16[576,896]{1,0:T(8,128)(2,1)} %bitcast.19, bf16[1,1024,896]{2,1,0:T(8,128)(2,1)S(1)} %copy-done), kind=kOutput, calls=%fused_computation.15 | convolution fusion | flops 1057554432 | bytes 4046848 | tf_op jit(solution)/shard_map/dot_general | solution.py:266
  110.8 20.1 %all-to-all-done.4.first_ref = bf16[8,448,256]{2,1,0:T(8,128)(2,1)} async-done(((bf16[8,448,256]{2,1,0:T(8,128)(2,1)}), bf16[8,448,256]{2,1,0:T(8,128)(2,1)}, u32[]{:S(2)}, u32[]{:S(2)}) %all-to-all-start.4) | async-done | bytes 1835040 | tf_op jit(solution)/shard_map/all_to_all | solution.py:229
  130.9 4.4 %all-to-all-start.5 = ((bf16[8,448,256]{2,1,0:T(8,128)(2,1)}), bf16[8,448,256]{2,1,0:T(8,128)(2,1)}, u32[]{:S(2)}, u32[]{:S(2)}) async-start(bf16[8,448,256]{2,1,0:T(8,128)(2,1)} %bitcast.76), calls=%async_computation.5 | async-start | bytes 3670016 | tf_op jit(solution)/shard_map/all_to_all | solution.py:229
  136.4 22.7 %all-to-all-done.5.second_ref = bf16[8,448,256]{2,1,0:T(8,128)(2,1)} async-done(((bf16[8,448,256]{2,1,0:T(8,128)(2,1)}), bf16[8,448,256]{2,1,0:T(8,128)(2,1)}, u32[]{:S(2)}, u32[]{:S(2)}) %all-to-all-start.5) | async-done | bytes 1835040 | tf_op jit(solution)/shard_map/all_to_all | solution.py:229
  159.1 3.6 %multiply_convert_fusion = bf16[576,896]{1,0:T(8,128)(2,1)} fusion(bf16[576,1024]{1,0:T(8,128)(2,1)} %all-gather.5.cloned.1.call-done, bf16[1,1024,896]{2,1,0:T(8,128)(2,1)S(1)} %copy-done), kind=kOutput, calls=%fused_computation.5 | convolution fusion | flops 1057996800 | bytes 4046848 | tf_op jit(solution)/shard_map/dot_general | solution.py:251
  162.8 3.6 %all-to-all-start.6 = ((bf16[8,72,896]{2,1,0:T(8,128)(2,1)}), bf16[8,72,896]{2,1,0:T(8,128)(2,1)S(1)}, u32[]{:S(2)}, u32[]{:S(2)}) async-start(bf16[8,72,896]{2,1,0:T(8,128)(2,1)} %bitcast.77), calls=%async_computation.6 | async-start | bytes 2064384 | tf_op jit(solution)/shard_map/all_to_all | solution.py:253
  166.9 4.4 %fusion = bf16[3584,256]{1,0:T(8,128)(2,1)S(1)} fusion(bf16[576,3584]{1,0:T(8,128)(2,1)} %copy-done.13, f32[576,256]{1,0:T(8,128)} %copy-done.16, f32[576,256]{1,0:T(8,128)} %get-tuple-element.49, bf16[576,256]{1,0:T(8,128)(2,1)} %reduce-scatter.2.cloned.1.call-done), kind=kOutput, calls=%fused_computation.4 | convolution fusion | flops 1060569088 | bytes 7438336 | tf_op jit(solution)/shard_map/dot_general | solution.py:283
  171.4 90.1 %shard_map.138 = (bf16[8,448,256]{2,1,0:T(8,128)(2,1)S(1)}, bf16[8,448,256]{2,1,0:T(8,128)(2,1)S(1)}, bf16[8,448,256]{2,1,0:T(8,128)(2,1)S(1)}) custom-call(s32[8]{0:T(128)S(1)} %copy-done.6, s32[8]{0:T(128)S(1)} %copy-done.7, bf16[8,448,256]{2,1,0:T(8,128)(2,1)} %all-to-all-done.3.weight_ref, bf16[8,448,256]{2,1,0:T(8,128)(2,1)} %all-to-all-done.4.first_ref, ...), custom_call_target="tpu_custom_call" | custom-call | flops 27525120 | bytes 183500800 | tf_op jit(solution)/shard_map/pallas_call | solution.py:166
  261.5 1.3 copy-done.1
  267.9 1.6 add_convert_fusion
  269.6 3.0 %copy.34 = bf16[1,3584,256]{2,1,0:T(8,128)(2,1)} copy(bf16[1,3584,256]{2,1,0:T(8,128)(2,1)} %bitcast.63) | data formatting | bytes 3670016
  272.5 1.2 copy.35
  (76 shorter events, 19.9 us)
Async XLA Ops:
  7.2 100.0 %copy-start = (bf16[1,1024,896]{2,1,0:T(8,128)(2,1)S(1)}, bf16[1,1024,896]{2,1,0:T(8,128)(2,1)}, u32[]{:S(2)}) copy-start(bf16[1,1024,896]{2,1,0:T(8,128)(2,1)} %param.19) | copy-start | bytes 5505028
  7.2 10.9 %copy-start.14 = (f32[128,3]{0,1:T(4,128)S(1)}, f32[128,3]{0,1:T(4,128)}, u32[]{:S(2)}) copy-start(f32[128,3]{0,1:T(4,128)} %param.16) | copy-start | bytes 4612
  7.2 11.1 %copy-start.12 = (bf16[128,896]{1,0:T(8,128)(2,1)S(1)}, bf16[128,896]{1,0:T(8,128)(2,1)}, u32[]{:S(2)}) copy-start(bf16[128,896]{1,0:T(8,128)(2,1)} %param.14) | copy-start | bytes 688132
  12.8 17.2 %all-to-all-start = ((bf16[8,72,640]{2,1,0:T(8,128)(2,1)}), bf16[8,72,640]{2,1,0:T(8,128)(2,1)S(1)}, u32[]{:S(2)}, u32[]{:S(2)}) async-start(bf16[8,72,640]{2,1,0:T(8,128)(2,1)} %bitcast.2), calls=%async_computation | async-start | bytes 1474560 | tf_op jit(solution)/shard_map/all_to_all | solution.py:229
  18.0 75.5 %all-gather.3.cloned.1.call-start = ((), (), s32[]{:S(2)}) async-start(), calls=%async_computation.8 | async-start | bytes 3686400 | tf_op jit(solution)/shard_map/all_gather | solution.py:233
  18.3 17.0 %slice-start = ((bf16[128,896]{1,0:T(8,128)(2,1)}), bf16[128,256]{1,0:T(8,128)(2,1)S(1)}, s32[]{:S(2)}) async-start(bf16[128,896]{1,0:T(8,128)(2,1)} %param.13), calls=%async_computation.11 | async-start | bytes 131072 | tf_op jit(solution)/shard_map/slice | solution.py:222
  31.0 21.4 %all-to-all-start.1 = ((bf16[8,72,896]{2,1,0:T(8,128)(2,1)}), bf16[8,72,896]{2,1,0:T(8,128)(2,1)}, u32[]{:S(2)}, u32[]{:S(2)}) async-start(bf16[8,72,896]{2,1,0:T(8,128)(2,1)} %bitcast.4), calls=%async_computation.1 | async-start | bytes 2064384 | tf_op jit(solution)/shard_map/all_to_all | solution.py:229
  73.1 21.7 %copy-start.8 = (bf16[8,72,1024]{2,1,0:T(8,128)(2,1)S(1)}, bf16[8,72,1024]{2,1,0:T(8,128)(2,1)}, u32[]{:S(2)}) copy-start(bf16[8,72,1024]{2,1,0:T(8,128)(2,1)} %all_to_all.35) | copy-start | bytes 3538948
  73.1 29.6 %all-to-all-start.3 = ((bf16[8,448,256]{2,1,0:T(8,128)(2,1)}), bf16[8,448,256]{2,1,0:T(8,128)(2,1)}, u32[]{:S(2)}, u32[]{:S(2)}) async-start(bf16[8,448,256]{2,1,0:T(8,128)(2,1)} %bitcast.74), calls=%async_computation.3 | async-start | bytes 3670016 | tf_op jit(solution)/shard_map/all_to_all | solution.py:229
  77.6 81.5 %all-gather.5.cloned.1.call-start = ((), (), s32[]{:S(2)}) async-start(), calls=%async_computation.9 | async-start | bytes 1474560 | tf_op jit(solution)/shard_map/all_gather | solution.py:247
  93.5 2.7 copy-start.9
  96.2 1.5 copy-start.11
  97.7 2.0 copy-start.13
  97.7 2.8 %copy-start.15 = (bf16[1,3584,256]{2,1,0:T(8,128)(2,1)S(1)}, bf16[1,3584,256]{2,1,0:T(8,128)(2,1)}, u32[]{:S(2)}) copy-start(bf16[1,3584,256]{2,1,0:T(8,128)(2,1)} %param.18) | copy-start | bytes 5505028
  100.5 2.1 copy-start.16
  102.7 28.2 %all-to-all-start.4 = ((bf16[8,448,256]{2,1,0:T(8,128)(2,1)}), bf16[8,448,256]{2,1,0:T(8,128)(2,1)}, u32[]{:S(2)}, u32[]{:S(2)}) async-start(bf16[8,448,256]{2,1,0:T(8,128)(2,1)} %bitcast.75), calls=%async_computation.4 | async-start | bytes 3670016 | tf_op jit(solution)/shard_map/all_to_all | solution.py:229
  107.1 59.9 %reduce-scatter.2.cloned.1.call-start = ((), (), s32[]{:S(2)}) async-start(), calls=%async_computation.10 | async-start | bytes 1474560 | tf_op jit(solution)/shard_map/reduce_scatter | solution.py:273
  130.9 28.2 %all-to-all-start.5 = ((bf16[8,448,256]{2,1,0:T(8,128)(2,1)}), bf16[8,448,256]{2,1,0:T(8,128)(2,1)}, u32[]{:S(2)}, u32[]{:S(2)}) async-start(bf16[8,448,256]{2,1,0:T(8,128)(2,1)} %bitcast.76), calls=%async_computation.5 | async-start | bytes 3670016 | tf_op jit(solution)/shard_map/all_to_all | solution.py:229
  162.8 102.4 %all-to-all-start.6 = ((bf16[8,72,896]{2,1,0:T(8,128)(2,1)}), bf16[8,72,896]{2,1,0:T(8,128)(2,1)S(1)}, u32[]{:S(2)}, u32[]{:S(2)}) async-start(bf16[8,72,896]{2,1,0:T(8,128)(2,1)} %bitcast.77), calls=%async_computation.6 | async-start | bytes 2064384 | tf_op jit(solution)/shard_map/all_to_all | solution.py:253
  166.9 4.4 %copy-start.6 = (s32[8]{0:T(128)S(1)}, s32[8]{0:T(128)}, u32[]{:S(2)}) copy-start(s32[8]{0:T(128)} %placement_ref.1) | copy-start | bytes 100
  166.9 4.4 %copy-start.7 = (s32[8]{0:T(128)S(1)}, s32[8]{0:T(128)}, u32[]{:S(2)}) copy-start(s32[8]{0:T(128)} %plan_ref.1) | copy-start | bytes 100
  261.4 1.3 copy-start.1
  269.6 3.0 %copy-start.4 = (bf16[8,448,256]{2,1,0:T(8,128)(2,1)S(1)}, bf16[8,448,256]{2,1,0:T(8,128)(2,1)}, u32[]{:S(2)}) copy-start(bf16[8,448,256]{2,1,0:T(8,128)(2,1)} %copy-done.3) | copy-start | bytes 5505028
  272.5 2.2 copy-start.2
  (3 other events, 3.3 us)
Sparse Core Ops, SparseCore 0:
  31.1 62.3 all-gather.2
  102.8 31.2 all-gather.4
  137.0 27.4 reduce-scatter.1
